TPU v7x, 512 devices: a whole 4x8x8 slice. The times are simulated.
512 devices in a mesh: lat: 16 (over y_lo, x, core), lon: 32 (over y_hi, z).
Axes of the slice: x: 4, y: 8 (y_hi: 4, y_lo: 2; y = y_hi * 2 + y_lo), z: 8, core: 2. Of those that a mesh axis runs over, the one named last changes fastest.
Arguments:
- field: bfloat16 [128, 1024, 256], P('lat', 'lon'), may hold values from -6 to 6
- kernel: float32 [7, 7, 256], replicated, may hold values from -0.875 to 0.875
- gain: float32 [256], replicated, may hold values from 0.1 to 1.9
- w_in: bfloat16 [256, 1024], replicated, may hold values from -0.375 to 0.375
- b_in: float32 [1024], replicated, may hold values from -1 to 1
- w_out: bfloat16 [1024, 256], replicated, may hold values from -0.1875 to 0.1875
- layer_scale: float32 [256], replicated, may hold values from 0.3 to 1.5
- cotangent: bfloat16 [128, 1024, 256], P('lat', 'lon'), may hold values from -6 to 6
Outputs:
- block_out: bfloat16 [128, 1024, 256], P('lat', 'lon')
- grad_field: bfloat16 [128, 1024, 256], P('lat', 'lon')
- grad_kernel: float32 [7, 7, 256], replicated
- grad_gain: float32 [256], replicated
- grad_w_in: float32 [256, 1024], P(None, ('lat', 'lon'))
- grad_b_in: float32 [1024], replicated
- grad_w_out: float32 [1024, 256], P(('lat', 'lon'))
- grad_scale: float32 [256], replicated
All inputs are finite; a program needn't handle non-finite values.
Results may differ from a plain program's by a relative error of at most 0.013.
Values may be sent and summed in bfloat16 or wider, within the bound.
A program may use at most 64 MiB of HBM per device.

v0:
```python
import jax
import jax.numpy as jnp
from jax import lax
from jax.sharding import PartitionSpec as P

GELU_K = 0.7978845608028654
GELU_C = 0.044715
LN_EPSILON = 1e-06


def padded_2(cells, sides, width, closed):
    for axis, dim in sides:
        count = lax.axis_size(axis)
        ends = count if closed else count - 1
        head = lax.slice_in_dim(cells, 0, width, axis=dim)
        tail = lax.slice_in_dim(cells, cells.shape[dim] - width, cells.shape[dim], axis=dim)
        cells = jnp.concatenate(
            [
                lax.ppermute(tail, axis, [(i, (i + 1) % count) for i in range(ends)]),
                cells,
                lax.ppermute(head, axis, [((i + 1) % count, i) for i in range(ends)]),
            ],
            axis=dim,
        )
    return cells


def gelu_pair(pre_act):
    inner = GELU_K * (pre_act + GELU_C * pre_act * pre_act * pre_act)
    tanh_val = jnp.tanh(inner)
    value = 0.5 * pre_act * (1.0 + tanh_val)
    gelu_slope = 0.5 * (1.0 + tanh_val) + 0.5 * pre_act * (1.0 - tanh_val * tanh_val) * GELU_K * (
        1.0 + 3.0 * GELU_C * pre_act * pre_act
    )
    return (value, gelu_slope)


def depthwise(padded, kernel, grid_rows, grid_cols):
    summed = jnp.zeros((grid_rows, grid_cols, kernel.shape[2]), jnp.float32)
    for row_tap in range(7):
        for col_tap in range(7):
            summed = (
                summed
                + padded[row_tap : row_tap + grid_rows, col_tap : col_tap + grid_cols, :].astype(
                    jnp.float32
                )
                * kernel[row_tap, col_tap]
            )
    return summed


def kernel_terms(padded, d_conv, grid_rows, grid_cols):
    taps = []
    for row_tap in range(7):
        for col_tap in range(7):
            window = padded[row_tap : row_tap + grid_rows, col_tap : col_tap + grid_cols, :].astype(
                jnp.float32
            )
            taps.append(jnp.sum(window * d_conv, axis=(0, 1)))
    return jnp.stack(taps).reshape(7, 7, d_conv.shape[2])


def contract_rows(left, right):
    return lax.dot_general(
        left, right, (((0,), (0,)), ((), ())), preferred_element_type=jnp.float32
    )


def local(field, kernel, gain, w_in, b_in, w_out, layer_scale, cotangent):
    grid_rows, grid_cols, channels = field.shape
    widened = padded_2(field, (("lon", 1),), 3, True)
    padded = padded_2(widened, (("lat", 0),), 3, False)
    conv = depthwise(padded, kernel, grid_rows, grid_cols).reshape(-1, channels)
    row_mean = jnp.mean(conv, axis=-1, keepdims=True)
    centred = conv - row_mean
    inv_dev = lax.rsqrt(jnp.mean(centred * centred, axis=-1, keepdims=True) + LN_EPSILON)
    normed_hat = centred * inv_dev
    normed = (normed_hat * gain).astype(jnp.bfloat16)
    pre_act = jnp.dot(normed, w_in, preferred_element_type=jnp.float32) + b_in
    activated, gelu_slope = gelu_pair(pre_act)
    hidden = activated.astype(jnp.bfloat16)
    branch = jnp.dot(hidden, w_out, preferred_element_type=jnp.float32)
    flat_field = field.reshape(-1, channels)
    block_out = (flat_field.astype(jnp.float32) + layer_scale * branch).astype(jnp.bfloat16)
    cot_wide = cotangent.reshape(-1, channels).astype(jnp.float32)
    d_branch = (layer_scale * cot_wide).astype(jnp.bfloat16)
    g_scale = jnp.sum(cot_wide * branch, axis=0)
    g_out = contract_rows(hidden, d_branch)
    d_hidden = lax.dot_general(
        d_branch, w_out, (((1,), (1,)), ((), ())), preferred_element_type=jnp.float32
    )
    d_pre = d_hidden * gelu_slope
    d_pre_b = d_pre.astype(jnp.bfloat16)
    g_bias = jnp.sum(d_pre, axis=0)
    g_in_t = contract_rows(d_pre_b, normed)
    d_normed = lax.dot_general(
        d_pre_b, w_in, (((1,), (1,)), ((), ())), preferred_element_type=jnp.float32
    )
    g_gain = jnp.sum(d_normed * normed_hat, axis=0)
    scaled = d_normed * gain
    d_conv = inv_dev * (
        scaled
        - jnp.mean(scaled, axis=-1, keepdims=True)
        - normed_hat * jnp.mean(scaled * normed_hat, axis=-1, keepdims=True)
    )
    d_conv = d_conv.reshape(grid_rows, grid_cols, channels)
    grad_widened = padded_2(d_conv.astype(jnp.bfloat16), (("lon", 1),), 3, True).astype(
        d_conv.dtype
    )
    grad_padded = padded_2(grad_widened.astype(jnp.bfloat16), (("lat", 0),), 3, False).astype(
        grad_widened.dtype
    )
    back = depthwise(grad_padded, kernel[::-1, ::-1, :], grid_rows, grid_cols)
    grad_field = (cotangent.astype(jnp.float32) + back).astype(jnp.bfloat16)
    g_kernel = kernel_terms(padded, d_conv, grid_rows, grid_cols)
    sum_in, sum_out = (
        lax.psum_scatter(g_in_t, ("lat", "lon"), scatter_dimension=0, tiled=True),
        lax.psum_scatter(g_out, ("lat", "lon"), scatter_dimension=0, tiled=True),
    )
    sum_kernel, sum_gain, sum_bias, sum_scale = lax.psum(
        (g_kernel, g_gain, g_bias, g_scale), ("lat", "lon")
    )
    total_cells = grid_rows * grid_cols * lax.axis_size("lat") * lax.axis_size("lon")
    factor = 1.0 / jnp.sqrt(jnp.float32(total_cells))
    return (
        block_out.reshape(grid_rows, grid_cols, channels),
        grad_field,
        sum_kernel * factor,
        sum_gain * factor,
        (sum_in * factor).T,
        sum_bias * factor,
        sum_out * factor,
        sum_scale * factor,
    )


def solution(mesh):
    in_specs = (P("lat", "lon", None), P(), P(), P(), P(), P(), P(), P("lat", "lon", None))
    out_specs = (
        P("lat", "lon", None),
        P("lat", "lon", None),
        P(),
        P(),
        P(None, ("lat", "lon")),
        P(),
        P(("lat", "lon"), None),
        P(),
    )
    return jax.shard_map(local, mesh=mesh, in_specs=in_specs, out_specs=out_specs, check_vma=False)
```

profile of v0, /device:TPU:1, one launch (start us, length us, event | category | flops | bytes accessed | tf_op | source)
XLA Modules:
  0.0 440.5 jit_solution(9962175649058632075)
XLA Ops:
  7.2 0.9 fusion.167
  8.1 15.2 %collective-permute-start.1 = (bf16[8,3,256]{2,1,0:T(4,128)(2,1)S(1)}, bf16[8,3,256]{2,1,0:T(4,128)(2,1)S(1)}, u32[]{:S(2)}, u32[]{:S(2)}) collective-permute-start(bf16[8,3,256]{2,1,0:T(4,128)(2,1)S(1)} %get-tuple-element.91), channel_id=1, source_target_pairs={{1,0},{2,1},{3,2},{4,3},{5,4},{6,5},{7,6},{8,7},{9,8},{10,9},{11,1... | collective-permute-start | bytes 36872 | tf_op jit(solution)/shard_map/ppermute | solution.py:21
  23.3 1.9 collective-permute-start
  25.2 0.9 fusion.170
  26.1 1.0 fusion.168
  27.1 1.0 fusion.169
  28.2 3.8 collective-permute-done
  32.0 5.1 %collective-permute-start.2 = (bf16[3,38,256]{2,1,0:T(8,128)(2,1)S(1)}, bf16[3,38,256]{2,1,0:T(8,128)(2,1)S(1)}, u32[]{:S(2)}, u32[]{:S(2)}) collective-permute-start(bf16[3,38,256]{2,1,0:T(8,128)(2,1)S(1)} %get-tuple-element.85), channel_id=1, source_target_pairs={{0,32},{32,64},{64,96},{96,128},{128,160},{160,192},{192,224},{224... | collective-permute-start | bytes 175112 | tf_op jit(solution)/shard_map/ppermute | solution.py:19
  37.2 1.9 collective-permute-start.3
  39.1 3.6 collective-permute-done.3
  42.8 1.9 fusion.164
  45.2 0.5 copy-done.2
  46.1 0.6 copy-done.3
  46.7 1.1 fusion.152
  47.8 0.8 fusion.171
  49.1 1.3 fusion.155
  50.5 1.6 fusion.162
  52.0 0.6 fusion.100
  53.2 2.9 collective-permute-start.5
  56.2 2.3 collective-permute-start.4
  58.5 0.5 fusion.82
  59.2 98.2 %all-reduce.2 = (f32[7,7,256]{2,1,0:T(8,128)S(1)}, f32[256]{0:T(256)S(1)}, f32[1024]{0:T(1024)S(1)}, f32[256]{0:T(256)S(1)}) all-reduce(f32[7,7,256]{2,1,0:T(8,128)S(1)} %reshape.80, f32[256]{0:T(256)S(1)} %get-tuple-element.8, f32[1024]{0:T(1024)S(1)} %get-tuple-element.142, ...), channel_id=1, replica_groups=mesh['lat'=16,'lon'=32] {'lat','lon'}, use_global_device_ids=true, to_apply=%region_53.0 | all-reduce | flops 14080 | bytes 112640 | tf_op jit(solution)/shard_map/psum | solution.py:120
  157.4 0.6 broadcast_multiply_fusion
  158.1 0.6 broadcast_multiply_fusion.1
  158.7 0.6 broadcast_multiply_fusion.4
  159.3 2.6 collective-permute-start.7
  161.9 3.0 collective-permute-start.6
  164.9 0.6 broadcast_multiply_fusion.3
  165.5 0.7 collective-permute-done.6
  166.2 2.2 fusion.103
  168.5 263.9 %all-reduce.6.cloned.1.call-done = (f32[1024,256]{1,0:T(8,128)}, f32[1024,256]{1,0:T(8,128)}) async-done(((f32[1024,256]{1,0:T(8,128)}, f32[1024,256]{1,0:T(8,128)}), (f32[1024,256]{1,0:T(8,128)}, f32[1024,256]{1,0:T(8,128)})) %all-reduce.6.cloned.1.call-update) | async-done | bytes 2097168
  432.4 1.3 dynamic-slice_multiply_fusion
  (39 shorter events, 2.4 us)
Async XLA Ops:
  7.2 38.9 %copy-start = (bf16[1024,256]{1,0:T(8,128)(2,1)S(1)}, bf16[1024,256]{1,0:T(8,128)(2,1)}, u32[]{:S(2)}) copy-start(bf16[1024,256]{1,0:T(8,128)(2,1)} %param.13) | copy-start | bytes 1572868
  7.2 21.0 %copy-start.1 = (bf16[8,32,256]{2,1,0:T(8,128)(2,1)S(1)}, bf16[8,32,256]{2,1,0:T(8,128)(2,1)}, u32[]{:S(2)}) copy-start(bf16[8,32,256]{2,1,0:T(8,128)(2,1)} %param.8) | copy-start | bytes 393220
  7.2 425.2 %all-reduce.6.cloned.1.call-start = ((), (), s32[]{:S(2)}) async-start(), calls=%async_computation | async-start | bytes 4194304
  8.1 20.1 %collective-permute-start.1 = (bf16[8,3,256]{2,1,0:T(4,128)(2,1)S(1)}, bf16[8,3,256]{2,1,0:T(4,128)(2,1)S(1)}, u32[]{:S(2)}, u32[]{:S(2)}) collective-permute-start(bf16[8,3,256]{2,1,0:T(4,128)(2,1)S(1)} %get-tuple-element.91), channel_id=1, source_target_pairs={{1,0},{2,1},{3,2},{4,3},{5,4},{6,5},{7,6},{8,7},{9,8},{10,9},{11,1... | collective-permute-start | bytes 36872 | tf_op jit(solution)/shard_map/ppermute | solution.py:21
  23.3 8.7 %collective-permute-start = (bf16[8,3,256]{2,1,0:T(4,128)(2,1)S(1)}, bf16[8,3,256]{2,1,0:T(4,128)(2,1)S(1)}, u32[]{:S(2)}, u32[]{:S(2)}) collective-permute-start(bf16[8,3,256]{2,1,0:T(4,128)(2,1)S(1)} %get-tuple-element.90), channel_id=1, source_target_pairs={{0,1},{1,2},{2,3},{3,4},{4,5},{5,6},{6,7},{7,8},{8,9},{9,10},{10,1... | collective-permute-start | bytes 36872 | tf_op jit(solution)/shard_map/ppermute | solution.py:19
  32.0 7.1 %collective-permute-start.2 = (bf16[3,38,256]{2,1,0:T(8,128)(2,1)S(1)}, bf16[3,38,256]{2,1,0:T(8,128)(2,1)S(1)}, u32[]{:S(2)}, u32[]{:S(2)}) collective-permute-start(bf16[3,38,256]{2,1,0:T(8,128)(2,1)S(1)} %get-tuple-element.85), channel_id=1, source_target_pairs={{0,32},{32,64},{64,96},{96,128},{128,160},{160,192},{192,224},{224... | collective-permute-start | bytes 175112 | tf_op jit(solution)/shard_map/ppermute | solution.py:19
  37.2 5.5 %collective-permute-start.3 = (bf16[3,38,256]{2,1,0:T(8,128)(2,1)S(1)}, bf16[3,38,256]{2,1,0:T(8,128)(2,1)S(1)}, u32[]{:S(2)}, u32[]{:S(2)}) collective-permute-start(bf16[3,38,256]{2,1,0:T(8,128)(2,1)S(1)} %get-tuple-element.86), channel_id=1, source_target_pairs={{32,0},{64,32},{96,64},{128,96},{160,128},{192,160},{224,192},{256... | collective-permute-start | bytes 175112 | tf_op jit(solution)/shard_map/ppermute | solution.py:21
  42.8 2.3 copy-start.4
  44.7 1.0 copy-start.2
  45.1 0.7 copy-start.5
  45.8 0.9 copy-start.3
  45.8 0.9 copy-start.6
  53.2 106.0 %collective-permute-start.5 = (bf16[8,3,256]{2,1,0:T(4,128)(2,1)S(1)}, bf16[8,3,256]{2,1,0:T(4,128)(2,1)S(1)}, u32[]{:S(2)}, u32[]{:S(2)}) collective-permute-start(bf16[8,3,256]{2,1,0:T(4,128)(2,1)S(1)} %get-tuple-element.89), channel_id=1, source_target_pairs={{1,0},{2,1},{3,2},{4,3},{5,4},{6,5},{7,6},{8,7},{9,8},{10,9},{11,1... | collective-permute-start | bytes 36872 | tf_op jit(solution)/shard_map/ppermute | solution.py:21
  56.2 103.1 %collective-permute-start.4 = (bf16[8,3,256]{2,1,0:T(4,128)(2,1)S(1)}, bf16[8,3,256]{2,1,0:T(4,128)(2,1)S(1)}, u32[]{:S(2)}, u32[]{:S(2)}) collective-permute-start(bf16[8,3,256]{2,1,0:T(4,128)(2,1)S(1)} %get-tuple-element.88), channel_id=1, source_target_pairs={{0,1},{1,2},{2,3},{3,4},{4,5},{5,6},{6,7},{7,8},{8,9},{9,10},{10,1... | collective-permute-start | bytes 36872 | tf_op jit(solution)/shard_map/ppermute | solution.py:19
  159.3 6.1 %collective-permute-start.7 = (bf16[3,38,256]{2,1,0:T(8,128)(2,1)S(1)}, bf16[3,38,256]{2,1,0:T(8,128)(2,1)S(1)}, u32[]{:S(2)}, u32[]{:S(2)}) collective-permute-start(bf16[3,38,256]{2,1,0:T(8,128)(2,1)S(1)} %get-tuple-element.82), channel_id=1, source_target_pairs={{32,0},{64,32},{96,64},{128,96},{160,128},{192,160},{224,192},{256... | collective-permute-start | bytes 175112 | tf_op jit(solution)/shard_map/ppermute | solution.py:21
  161.9 4.3 collective-permute-start.6
Sparse Core Ops, SparseCore 0:
  159.4 272.9 all-reduce.5
where the time goes:
time: 441 us; the launch traced here: 440 us
  waiting for transfers between devices  272 us (62%)
  blocking collectives  98.2 us (22%)
  starting transfers between devices  35 us (8%)
  between operations  14.3 us (3%)
  other arithmetic  10 us (2%)
  matrix products  5.63 us (1%)
  local copies, waits for them, and re-layouts  5.35 us (1%)
    unnamed x2, waiting for transfers between devices  264 us
    psum x1, blocking collectives, local(): lax.psum((g_kernel, g_gain, g_bias, g_scale), ('lat', 'lon'))  98.2 us
    ppermute x4, starting transfers between devices, padded_2(): lax.ppermute(head, axis, [((i + 1) % count, i) for i in range(ends)])  22.6 us
    ppermute x4, starting transfers between devices, padded_2(): lax.ppermute(tail, axis, [(i, (i + 1) % count) for i in range(ends)])  12.4 us
  transfers between devices with their start and end apart: 9, of which 4 were waited for; matrix products, arithmetic and copies ran while one was open for 2% of the time, Pallas kernels for 0%

commit v1 on v0

v1 whole, which is shorter than its diff:
```python
import jax
import jax.numpy as jnp
from jax import lax
from jax.experimental import pallas as pl
from jax.experimental.pallas import tpu as pltpu
from jax.sharding import PartitionSpec as P

GELU_K = 0.7978845608028654
GELU_C = 0.044715
LN_EPSILON = 1e-06
F32 = jnp.float32
BF16 = jnp.bfloat16
MESH = pl.DeviceIdType.MESH

N_X, N_Y, N_Z = 4, 8, 8
N_LAT, N_LON = 16, 32
ROWS, COLS, CH, FF = 8, 32, 256, 1024
CELLS = ROWS * COLS
HALF = 128
LEFT = 8
CHUNKS = 4
CHUNK = FF // CHUNKS
SUMS = 64
FACTOR = 1.0 / 131072.0**0.5


def dot(left, right, over_left, over_right):
    return lax.dot_general(
        left, right, (((over_left,), (over_right,)), ((), ())), preferred_element_type=F32
    )


class Place:
    def __init__(self):
        self.lat = lax.axis_index("lat")
        self.lon = lax.axis_index("lon")
        self.core = lax.rem(self.lat, 2)
        self.x = lax.rem(self.lat // 2, N_X)
        self.y_lo = self.lat // 8
        self.z = lax.rem(self.lon, N_Z)
        self.y_hi = self.lon // N_Z
        self.y = self.y_hi * 2 + self.y_lo

    def grid(self, down, right):
        return (
            lax.rem(self.lat + down + N_LAT, N_LAT),
            lax.rem(self.lon + right + N_LON, N_LON),
        )

    def sibling(self):
        return (self.lat + 1 - 2 * self.core, self.lon)

    def on_x(self, x):
        return (self.y_lo * 8 + x * 2 + self.core, self.lon)

    def on_y(self, y):
        return (lax.rem(y, 2) * 8 + self.x * 2 + self.core, (y // 2) * N_Z + self.z)

    def on_z(self, z):
        return (self.lat, self.y_hi * N_Z + z)


def remote(src, dst, send, recv, device):
    return pltpu.make_async_remote_copy(
        src_ref=src, dst_ref=dst, send_sem=send, recv_sem=recv, device_id=device, device_id_type=MESH
    )


SIDES = ((-1, 0), (1, 0), (0, -1), (0, 1), (-1, -1), (-1, 1), (1, -1), (1, 1))


def halo_pack(pad, tmp, rows_out, cols_out):
    for half in range(2):
        lanes = slice(half * HALF, (half + 1) * HALF)
        rows_out[0, :, :, lanes] = pad[half, 3:6, LEFT : LEFT + COLS, :].astype(BF16)
        rows_out[1, :, :, lanes] = pad[half, 8:11, LEFT : LEFT + COLS, :].astype(BF16)
        for row in range(ROWS):
            tmp[0, row * 4 : row * 4 + 4, lanes] = pad[half, 3 + row, LEFT : LEFT + 4, :]
            tmp[1, row * 4 : row * 4 + 4, lanes] = pad[half, 3 + row, LEFT + 28 : LEFT + 32, :]
    cols_out[...] = tmp[...].astype(BF16)


def halo_copies(place, rows_out, cols_out, rows_in, cols_in, corners_in, send, recv):
    pairs = (
        (rows_out.at[0], rows_in.at[1]),
        (rows_out.at[1], rows_in.at[0]),
        (cols_out.at[0], cols_in.at[1]),
        (cols_out.at[1], cols_in.at[0]),
        (cols_out.at[0, 0:16], corners_in.at[3]),
        (cols_out.at[1, 0:16], corners_in.at[2]),
        (cols_out.at[0, 16:32], corners_in.at[1]),
        (cols_out.at[1, 16:32], corners_in.at[0]),
    )
    return [
        remote(src, dst, send.at[at], recv.at[at], place.grid(*SIDES[at]))
        for at, (src, dst) in enumerate(pairs)
    ]


def halo_unpack(place, pad, rows_in, cols_in, corners_in):
    above = jnp.where(place.lat == 0, 0.0, 1.0).astype(F32)
    below = jnp.where(place.lat == N_LAT - 1, 0.0, 1.0).astype(F32)
    for half in range(2):
        lanes = slice(half * HALF, (half + 1) * HALF)
        pad[half, 0:3, LEFT : LEFT + COLS, :] = rows_in[0, :, :, lanes].astype(F32) * above
        pad[half, 11:14, LEFT : LEFT + COLS, :] = rows_in[1, :, :, lanes].astype(F32) * below
        for side, at in ((0, LEFT - 4), (1, LEFT + COLS)):
            wide = cols_in[side, :, lanes].astype(F32)
            for row in range(ROWS):
                pad[half, 3 + row, at : at + 4, :] = wide[row * 4 : row * 4 + 4]
            top = corners_in[side, :, lanes].astype(F32) * above
            bottom = corners_in[2 + side, :, lanes].astype(F32) * below
            for row in range(3):
                pad[half, row, at : at + 4, :] = top[4 + row * 4 : 8 + row * 4]
                pad[half, 11 + row, at : at + 4, :] = bottom[row * 4 : row * 4 + 4]


def depthwise(pad, taps, out, flipped):
    def one_half(half, carry):
        lanes = pl.ds(pl.multiple_of(half * HALF, HALF), HALF)
        for col in range(0, COLS, 8):
            summed = jnp.zeros((ROWS, 8, HALF), F32)
            for b in range(7):
                start = LEFT - 3 + b + col
                window = pad[half, :, start : start + 8, :]
                for a in range(7):
                    at = (6 - a, 6 - b) if flipped else (a, b)
                    tap = taps[at[0], at[1] : at[1] + 1, lanes]
                    summed = summed + window[a : a + ROWS] * tap[None]
            out[half, :, col : col + 8, :] = summed
        return carry

    lax.fori_loop(0, 2, one_half, 0)


def tap_sums(pad, d_pad, sums):
    def one_half(half, carry):
        lanes = pl.ds(pl.multiple_of(half * HALF, HALF), HALF)
        for b in range(7):
            totals = [jnp.zeros((8, HALF), F32) for _ in range(7)]
            for col in range(0, COLS, 8):
                start = LEFT - 3 + b + col
                window = pad[half, :, start : start + 8, :]
                grads = d_pad[half, 3 : 3 + ROWS, LEFT + col : LEFT + col + 8, :]
                for a in range(7):
                    totals[a] = totals[a] + jnp.sum(window[a : a + ROWS] * grads, axis=0)
            for a in range(7):
                at = a * 7 + b
                sums[at : at + 1, lanes] = jnp.sum(totals[a], axis=0, keepdims=True)
        return carry

    lax.fori_loop(0, 2, one_half, 0)


def gelu_pair(pre_act):
    square = pre_act * pre_act
    tanh_val = jnp.tanh(GELU_K * pre_act * (1.0 + GELU_C * square))
    half_up = 0.5 + 0.5 * tanh_val
    value = pre_act * half_up
    gelu_slope = half_up + value * (1.0 - tanh_val) * (GELU_K + (3.0 * GELU_C * GELU_K) * square)
    return value, gelu_slope


def step(
    field, taps, gain, w_in, b_in, w_out, layer_scale, cotangent,
    block_out, grad_field, small_out, large_out,
    pad, d_pad, conv, hat, normed, d_branch, inv_all, tmp,
    rows_out, cols_out, rows_in, cols_in, corners_in,
    d_rows_out, d_cols_out, d_rows_in, d_cols_in, d_corners_in,
    part, part_in, x_out, x_in, y_out, y_in, z_out, z_in,
    sums, sums_out, sums_in, sx, sy_a, sz_b, sz_a, sy_b, s_final,
    halo_send, halo_recv, d_halo_send, d_halo_recv,
    core_send, core_recv, x_send, x_recv, y_send, y_recv, z_send, z_recv,
    s_core_send, s_core_recv, sx_send, sx_recv, s3_send, s3_recv, s4_send, s4_recv, s_all_send, s_all_recv,
):
    place = Place()
    core, x, y, z = place.core, place.x, place.y, place.z

    barrier = pltpu.get_barrier_semaphore()
    partners = [place.grid(*side) for side in SIDES]
    partners.append(place.sibling())
    partners += [place.on_x(lax.rem(x + k, N_X)) for k in range(1, N_X)]
    partners += [place.on_y(lax.rem(y + k, N_Y)) for k in range(1, N_Y)]
    partners += [place.on_z(lax.rem(z + k, N_Z)) for k in range(1, N_Z)]
    for device in partners:
        pl.semaphore_signal(barrier, inc=1, device_id=device, device_id_type=MESH)

    for half in range(2):
        lanes = slice(half * HALF, (half + 1) * HALF)
        pad[half, 3 : 3 + ROWS, LEFT : LEFT + COLS, :] = field[:, :, lanes].astype(F32)
    halo_pack(pad, tmp, rows_out, cols_out)
    wide_cot = cotangent[...].reshape(CELLS, CH).astype(F32)
    d_branch[...] = (layer_scale[...] * wide_cot).astype(BF16)

    pl.semaphore_wait(barrier, len(partners))
    halos = halo_copies(place, rows_out, cols_out, rows_in, cols_in, corners_in, halo_send, halo_recv)
    for copy in halos:
        copy.start()
    for copy in halos:
        copy.wait()
    halo_unpack(place, pad, rows_in, cols_in, corners_in)

    depthwise(pad, taps, conv, False)
    parts = [conv[half].reshape(CELLS, HALF) for half in range(2)]
    mean = jnp.sum(parts[0] + parts[1], axis=-1, keepdims=True) * (1.0 / CH)
    parts = [value - mean for value in parts]
    spread = jnp.sum(parts[0] * parts[0] + parts[1] * parts[1], axis=-1, keepdims=True) * (1.0 / CH)
    inv_dev = lax.rsqrt(spread + LN_EPSILON)
    inv_all[...] = jnp.broadcast_to(inv_dev, (CELLS, HALF))
    for half in range(2):
        lanes = slice(half * HALF, (half + 1) * HALF)
        value = parts[half] * inv_dev
        hat[half] = value
        normed[:, lanes] = (value * gain[:, lanes]).astype(BF16)

    branch = jnp.zeros((CELLS, CH), F32)
    d_normed = jnp.zeros((CELLS, CH), F32)
    core_copies = []
    for chunk in range(CHUNKS):
        hidden_units = slice(chunk * CHUNK, (chunk + 1) * CHUNK)
        pre_act = dot(normed[...], w_in[:, hidden_units], 1, 0) + b_in[:, hidden_units]
        value, gelu_slope = gelu_pair(pre_act)
        hidden = value.astype(BF16)
        d_pre = dot(d_branch[...], w_out[hidden_units, :], 1, 1) * gelu_slope
        d_pre_b = d_pre.astype(BF16)
        part[1, chunk] = dot(hidden, d_branch[...], 0, 0).astype(BF16).reshape(2, 2, 64, CH)
        part[0, chunk] = dot(d_pre_b, normed[...], 0, 0).astype(BF16).reshape(2, 2, 64, CH)
        for which in (1, 0):
            copy = remote(
                part.at[which, chunk, :, 1 - core], part_in.at[which, chunk],
                core_send.at[which, chunk], core_recv.at[which, chunk], place.sibling(),
            )
            copy.start()
            core_copies.append((which, chunk, copy))
        branch = branch + dot(hidden, w_out[hidden_units, :], 1, 0)
        d_normed = d_normed + dot(d_pre_b, w_in[:, hidden_units], 1, 1)
        sums[51 + chunk : 52 + chunk, :] = jnp.sum(d_pre, axis=0, keepdims=True)

    wide_cot = cotangent[...].reshape(CELLS, CH).astype(F32)
    sums[50:51, :] = jnp.sum(wide_cot * branch, axis=0, keepdims=True)
    sums[55:64, :] = jnp.zeros((9, CH), F32)
    block_out[...] = (
        field[...].reshape(CELLS, CH).astype(F32) + layer_scale[...] * branch
    ).astype(BF16).reshape(ROWS, COLS, CH)

    hats = [hat[half] for half in range(2)]
    d_halves = [d_normed[:, half * HALF : (half + 1) * HALF] for half in range(2)]
    scaled = []
    for half in range(2):
        lanes = slice(half * HALF, (half + 1) * HALF)
        sums[49:50, lanes] = jnp.sum(d_halves[half] * hats[half], axis=0, keepdims=True)
        scaled.append(d_halves[half] * gain[:, lanes])
    m1 = jnp.sum(scaled[0] + scaled[1], axis=-1, keepdims=True) * (1.0 / CH)
    m2 = jnp.sum(scaled[0] * hats[0] + scaled[1] * hats[1], axis=-1, keepdims=True) * (1.0 / CH)
    for half in range(2):
        d_conv = inv_all[...] * (scaled[half] - m1 - hats[half] * m2)
        d_pad[half, 3 : 3 + ROWS, LEFT : LEFT + COLS, :] = d_conv.reshape(ROWS, COLS, HALF)

    halo_pack(d_pad, tmp, d_rows_out, d_cols_out)
    d_halos = halo_copies(
        place, d_rows_out, d_cols_out, d_rows_in, d_cols_in, d_corners_in, d_halo_send, d_halo_recv
    )
    for copy in d_halos:
        copy.start()

    x_copies = []
    for which, chunk, copy in core_copies:
        copy.wait()
        both = part[which, chunk, :, core].astype(F32) + part_in[which, chunk].astype(F32)
        x_out[which, chunk // 2, (chunk % 2) * 2 : (chunk % 2) * 2 + 2] = both.astype(BF16)
    for which in (1, 0):
        for k in range(1, N_X):
            to = lax.rem(x + k, N_X)
            copy = remote(
                x_out.at[which, :, to], x_in.at[which, k - 1],
                x_send.at[which, k - 1], x_recv.at[which, k - 1], place.on_x(to),
            )
            copy.start()
            x_copies.append(copy)

    tap_sums(pad, d_pad, sums)

    sums_out[...] = sums[...].reshape(2, SUMS // 2, CH).astype(BF16)
    s_core = remote(sums_out.at[1 - core], sums_in, s_core_send, s_core_recv, place.sibling())
    s_core.start()

    y_copies = []
    for which in (1, 0):
        total = x_out[which, :, x].astype(F32)
        for k in range(1, N_X):
            x_copies[(1 - which) * (N_X - 1) + k - 1].wait()
            total = total + x_in[which, k - 1].astype(F32)
        y_out[which] = total.astype(BF16).reshape(2, 4, 16, CH)
        if which == 1:
            s_core.wait()
            sx[x] = (sums_out[core].astype(F32) + sums_in[...].astype(F32)).astype(BF16)
            sx_copies = []
            for k in range(1, N_X):
                to = lax.rem(x + k, N_X)
                copy = remote(sx.at[x], sx.at[x], sx_send.at[to], sx_recv.at[x], place.on_x(to))
                copy.start()
                sx_copies.append(copy)
        for k in range(1, N_Y):
            to = lax.rem(y + k, N_Y)
            copy = remote(
                y_out.at[which, lax.rem(to, 2), to // 2], y_in.at[which, k - 1],
                y_send.at[which, k - 1], y_recv.at[which, k - 1], place.on_y(to),
            )
            copy.start()
            y_copies.append(copy)

    def gather_sum(slots, count):
        total = slots[0].astype(F32)
        for at in range(1, count):
            total = total + slots[at].astype(F32)
        return total

    def wait_slots(slots, send, recv, own, count, device_on):
        for k in range(1, count):
            other = lax.rem(own + k, count)
            remote(slots.at[own], slots.at[other], send.at[other], recv.at[other], device_on(other)).wait()

    def share(slots, send, recv, own, count, device_on):
        for k in range(1, count):
            other = lax.rem(own + k, count)
            remote(slots.at[own], slots.at[own], send.at[other], recv.at[own], device_on(other)).start()

    wait_slots(sx, sx_send, sx_recv, x, N_X, place.on_x)
    total = gather_sum(sx, N_X).astype(BF16)
    sy_a[y] = total[0:16]
    sz_b[z] = total[16:32]
    share(sy_a, s3_send.at[0], s3_recv.at[0], y, N_Y, place.on_y)
    share(sz_b, s3_send.at[1], s3_recv.at[1], z, N_Z, place.on_z)

    for copy in d_halos:
        copy.wait()
    halo_unpack(place, d_pad, d_rows_in, d_cols_in, d_corners_in)
    depthwise(d_pad, taps, conv, True)
    for half in range(2):
        lanes = slice(half * HALF, (half + 1) * HALF)
        grad_field[:, :, lanes] = (cotangent[:, :, lanes].astype(F32) + conv[half]).astype(BF16)

    for which in (1, 0):
        total = y_out[which, place.y_lo, place.y_hi].astype(F32)
        for k in range(1, N_Y):
            y_copies[(1 - which) * (N_Y - 1) + k - 1].wait()
            total = total + y_in[which, k - 1].astype(F32)
        for to in range(N_Z):
            for half in range(2):
                at = which * 4 + half * 2
                z_out[to, at : at + 2, :] = total[2 * to : 2 * to + 2, half * HALF : (half + 1) * HALF]
    z_copies = []
    for k in range(1, N_Z):
        to = lax.rem(z + k, N_Z)
        copy = remote(z_out.at[to], z_in.at[k - 1], z_send.at[k - 1], z_recv.at[k - 1], place.on_z(to))
        copy.start()
        z_copies.append(copy)

    wait_slots(sy_a, s3_send.at[0], s3_recv.at[0], y, N_Y, place.on_y)
    wait_slots(sz_b, s3_send.at[1], s3_recv.at[1], z, N_Z, place.on_z)
    sz_a[z] = gather_sum(sy_a, N_Y).astype(BF16)
    sy_b[y] = gather_sum(sz_b, N_Z).astype(BF16)
    share(sz_a, s4_send.at[0], s4_recv.at[0], z, N_Z, place.on_z)
    share(sy_b, s4_send.at[1], s4_recv.at[1], y, N_Y, place.on_y)

    total = z_out[z]
    for k in range(1, N_Z):
        z_copies[k - 1].wait()
        total = total + z_in[k - 1]
    large_out[...] = total * FACTOR

    wait_slots(sz_a, s4_send.at[0], s4_recv.at[0], z, N_Z, place.on_z)
    wait_slots(sy_b, s4_send.at[1], s4_recv.at[1], y, N_Y, place.on_y)
    s_final[core, 0:16] = gather_sum(sz_a, N_Z) * FACTOR
    s_final[core, 16:32] = gather_sum(sy_b, N_Y) * FACTOR
    s_all = remote(s_final.at[core], s_final.at[core], s_all_send, s_all_recv, place.sibling())
    s_all.start()
    s_all.wait_send()
    remote(s_final.at[core], s_final.at[1 - core], s_all_send, s_all_recv, place.sibling()).wait_recv()
    small_out[...] = s_final[...].reshape(SUMS, CH)


def finish(
    block_in, field_in, small, large,
    block_out, grad_field, grad_taps, grad_gain, grad_in, grad_bias, grad_out, grad_scale,
):
    block_out[...] = block_in[...]
    grad_field[...] = field_in[...]
    for a in range(7):
        grad_taps[a] = small[a * 7 : a * 7 + 7, :]
    grad_gain[...] = small[49:50, :]
    grad_scale[...] = small[50:51, :]
    for chunk in range(CHUNKS):
        grad_bias[:, chunk * CHUNK : (chunk + 1) * CHUNK] = small[51 + chunk : 52 + chunk, :]
    for half in range(2):
        lanes = slice(half * HALF, (half + 1) * HALF)
        grad_in[:, lanes] = large[half * 2 : half * 2 + 2, :]
        grad_out[:, lanes] = large[4 + half * 2 : 6 + half * 2, :]


def local(field, kernel, gain, w_in, b_in, w_out, layer_scale, cotangent):
    vmem = pl.BlockSpec(memory_space=pltpu.VMEM)
    dma = pltpu.SemaphoreType.DMA
    halo = [
        pltpu.VMEM((2, 3, COLS, CH), BF16),
        pltpu.VMEM((2, 4 * ROWS, CH), BF16),
        pltpu.VMEM((2, 3, COLS, CH), BF16),
        pltpu.VMEM((2, 4 * ROWS, CH), BF16),
        pltpu.VMEM((4, 16, CH), BF16),
    ]
    scratch = [
        pltpu.VMEM((2, ROWS + 6, COLS + 16, HALF), F32),
        pltpu.VMEM((2, ROWS + 6, COLS + 16, HALF), F32),
        pltpu.VMEM((2, ROWS, COLS, HALF), F32),
        pltpu.VMEM((2, CELLS, HALF), F32),
        pltpu.VMEM((CELLS, CH), BF16),
        pltpu.VMEM((CELLS, CH), BF16),
        pltpu.VMEM((CELLS, HALF), F32),
        pltpu.VMEM((2, 4 * ROWS, CH), F32),
        *halo,
        *halo,
        pltpu.VMEM((2, CHUNKS, 2, 2, 64, CH), BF16),
        pltpu.VMEM((2, CHUNKS, 2, 64, CH), BF16),
        pltpu.VMEM((2, 2, N_X, 64, CH), BF16),
        pltpu.VMEM((2, N_X - 1, 2, 64, CH), BF16),
        pltpu.VMEM((2, 2, 4, 16, CH), BF16),
        pltpu.VMEM((2, N_Y - 1, 16, CH), BF16),
        pltpu.VMEM((N_Z, 8, HALF), F32),
        pltpu.VMEM((N_Z - 1, 8, HALF), F32),
        pltpu.VMEM((SUMS, CH), F32),
        pltpu.VMEM((2, SUMS // 2, CH), BF16),
        pltpu.VMEM((SUMS // 2, CH), BF16),
        pltpu.VMEM((N_X, SUMS // 2, CH), BF16),
        pltpu.VMEM((N_Y, 16, CH), BF16),
        pltpu.VMEM((N_Z, 16, CH), BF16),
        pltpu.VMEM((N_Z, 16, CH), BF16),
        pltpu.VMEM((N_Y, 16, CH), BF16),
        pltpu.VMEM((2, SUMS // 2, CH), F32),
        dma((8,)), dma((8,)), dma((8,)), dma((8,)),
        dma((2, CHUNKS)), dma((2, CHUNKS)),
        dma((2, N_X - 1)), dma((2, N_X - 1)),
        dma((2, N_Y - 1)), dma((2, N_Y - 1)),
        dma((N_Z - 1,)), dma((N_Z - 1,)),
        dma, dma,
        dma((N_X,)), dma((N_X,)),
        dma((2, 8)), dma((2, 8)), dma((2, 8)), dma((2, 8)),
        dma, dma,
    ]
    grid_shape = jax.ShapeDtypeStruct(field.shape, BF16)
    mids = pl.pallas_call(
        step,
        out_shape=(
            grid_shape,
            grid_shape,
            jax.ShapeDtypeStruct((SUMS, CH), F32),
            jax.ShapeDtypeStruct((8, HALF), F32),
        ),
        in_specs=[vmem] * 8,
        out_specs=[vmem] * 4,
        scratch_shapes=scratch,
        compiler_params=pltpu.CompilerParams(
            collective_id=0, has_side_effects=True, vmem_limit_bytes=48 * 2**20
        ),
        name="block_step",
    )(
        field, kernel, gain.reshape(1, CH), w_in, b_in.reshape(1, FF), w_out,
        layer_scale.reshape(1, CH), cotangent,
    )
    block_out, grad_field, g_kernel, g_gain, g_in, g_bias, g_out, g_scale = pl.pallas_call(
        finish,
        out_shape=(
            grid_shape,
            grid_shape,
            jax.ShapeDtypeStruct((7, 7, CH), F32),
            jax.ShapeDtypeStruct((1, CH), F32),
            jax.ShapeDtypeStruct((2, CH), F32),
            jax.ShapeDtypeStruct((1, FF), F32),
            jax.ShapeDtypeStruct((2, CH), F32),
            jax.ShapeDtypeStruct((1, CH), F32),
        ),
        in_specs=[vmem] * 4,
        out_specs=[vmem] * 8,
        name="write_outputs",
    )(*mids)
    return (
        block_out,
        grad_field,
        g_kernel,
        g_gain.reshape(CH),
        g_in.T,
        g_bias.reshape(FF),
        g_out,
        g_scale.reshape(CH),
    )


def solution(mesh):
    in_specs = (P("lat", "lon", None), P(), P(), P(), P(), P(), P(), P("lat", "lon", None))
    out_specs = (
        P("lat", "lon", None),
        P("lat", "lon", None),
        P(),
        P(),
        P(None, ("lat", "lon")),
        P(),
        P(("lat", "lon"), None),
        P(),
    )
    return jax.shard_map(local, mesh=mesh, in_specs=in_specs, out_specs=out_specs, check_vma=False)
```

time: 441 us -> 60.2 us (0.14)
  waiting for transfers between devices: 272 us -> 0 us
  blocking collectives: 98.2 us -> 0 us
  Pallas kernels: 0 us -> 50.6 us
  starting transfers between devices: 35 us -> 0 us
  between operations: 14.3 us -> 0.68 us
  other arithmetic: 10 us -> 0 us
  matrix products: 5.63 us -> 0 us
    unnamed x2 -> x0, waiting for transfers between devices: 264 us -> none
    psum x1 -> x0, blocking collectives: 98.2 us -> none  [local(): lax.psum((g_kernel, g_gain, g_bias, g_scale), ('lat', 'lon'))]
    pallas_call x0 -> x2, Pallas kernels: none -> 50.6 us  [the longest x1 48.9 us: local(): pl.pallas_call(step, out_shape=(grid_shape, grid_shape, jax.ShapeDtypeStr...]
    ppermute x8 -> x0, starting transfers between devices: 35 us -> none  [the longest x4 22.6 us: padded_2(): lax.ppermute(head, axis, [((i + 1) % count, i) for i in range(ends)])]
    ppermute x8 -> x0, waiting for transfers between devices: 8.08 us -> none  [the longest x4 4.5 us: padded_2(): lax.ppermute(tail, axis, [(i, (i + 1) % count) for i in range(ends)])]
    unnamed x15 -> x24, local copies, waits for them, and re-layouts: 1.2 us -> 8.56 us
    dot_general x6 -> x0, matrix products: 5.63 us -> none  [the longest x2 2.91 us: contract_rows(): lax.dot_general(left, right, (((0,), (0,)), ((), ())), preferred_element_...]
  transfers between devices with their start and end apart: 9 -> 0, of which waited for: 4 -> 0; matrix products, arithmetic and copies ran while one was open for 2% -> 0% of each run, Pallas kernels for 0% -> 0%
where the time goes in v1:
time: 60.2 us; the launch traced here: 59.8 us
  Pallas kernels  50.6 us (84%)
  local copies, waits for them, and re-layouts  8.56 us (14%)
  between operations  0.68 us (1%)
    pallas_call x1, Pallas kernels, local(): pl.pallas_call(step, out_shape=(grid_shape, grid_shape, jax.ShapeDtypeStr...  48.9 us
    unnamed x24, local copies, waits for them, and re-layouts  8.56 us
    pallas_call x1, Pallas kernels, local(): pl.pallas_call(finish, out_shape=(grid_shape, grid_shape, jax.ShapeDtypeS...  1.71 us

profile of v1, /device:TPU:1, one launch (start us, length us, event | category | flops | bytes accessed | tf_op | source)
XLA Modules:
  0.0 59.8 jit_solution(1402840052402557327)
XLA Ops:
  0.6 0.0 copy-start.8
  0.6 0.0 copy-start.10
  0.7 0.7 %copy-done.8 = f32[1024]{0:T(1024)S(1)} copy-done((f32[1024]{0:T(1024)S(1)}, f32[1024]{0:T(1024)}, u32[]{:S(2)}) %copy-start.8) | copy-done | bytes 4120
  1.3 0.0 copy-done.10
  1.3 0.0 copy-start
  1.3 1.0 %copy-done = bf16[256,1024]{1,0:T(8,128)(2,1)S(1)} copy-done((bf16[256,1024]{1,0:T(8,128)(2,1)S(1)}, bf16[256,1024]{1,0:T(8,128)(2,1)}, u32[]{:S(2)}) %copy-start) | copy-done | bytes 524312
  2.4 0.0 copy-start.1
  2.4 1.0 %copy-done.1 = bf16[1024,256]{1,0:T(8,128)(2,1)S(1)} copy-done((bf16[1024,256]{1,0:T(8,128)(2,1)S(1)}, bf16[1024,256]{1,0:T(8,128)(2,1)}, u32[]{:S(2)}) %copy-start.1) | copy-done | bytes 524312
  3.4 0.0 copy-start.4
  3.4 0.9 %copy-done.4 = bf16[8,32,256]{2,1,0:T(8,128)(2,1)S(1)} copy-done((bf16[8,32,256]{2,1,0:T(8,128)(2,1)S(1)}, bf16[8,32,256]{2,1,0:T(8,128)(2,1)}, u32[]{:S(2)}) %copy-start.4) | copy-done | bytes 131096
  4.3 0.0 copy-start.5
  4.3 0.9 %copy-done.5 = bf16[8,32,256]{2,1,0:T(8,128)(2,1)S(1)} copy-done((bf16[8,32,256]{2,1,0:T(8,128)(2,1)S(1)}, bf16[8,32,256]{2,1,0:T(8,128)(2,1)}, u32[]{:S(2)}) %copy-start.5) | copy-done | bytes 131096
  5.2 0.0 copy-start.7
  5.2 0.8 %copy-done.7 = f32[7,7,256]{2,1,0:T(8,128)S(1)} copy-done((f32[7,7,256]{2,1,0:T(8,128)S(1)}, f32[7,7,256]{2,1,0:T(8,128)}, u32[]{:S(2)}) %copy-start.7) | copy-done | bytes 50200
  6.0 0.0 copy-start.11
  6.0 0.7 %copy-done.11 = f32[256]{0:T(256)S(1)} copy-done((f32[256]{0:T(256)S(1)}, f32[256]{0:T(256)}, u32[]{:S(2)}) %copy-start.11) | copy-done | bytes 1048
  6.7 48.9 %block_step.1 = (bf16[8,32,256]{2,1,0:T(8,128)(2,1)S(1)}, bf16[8,32,256]{2,1,0:T(8,128)(2,1)S(1)}, f32[64,256]{1,0:T(8,128)S(1)}, f32[8,128]{1,0:T(8,128)S(1)}) custom-call(bf16[8,32,256]{2,1,0:T(8,128)(2,1)S(1)} %copy-done.4, f32[7,7,256]{2,1,0:T(8,128)S(1)} %copy-done.7, f32[1,256]{1,0:T(1,128)S(1)} %bitcast.8, bf16[256,1024]{1,0:T(8,128)(2,1)S(1)} %copy-done, ...), custom_call_target="tpu_custom_call" | custom-call | tf_op jit(solution)/shard_map/block_step/pallas_call | solution.py:450
  55.6 0.0 copy-start.2
  55.6 0.6 %copy-done.2 = bf16[8,32,256]{2,1,0:T(8,128)(2,1)} copy-done((bf16[8,32,256]{2,1,0:T(8,128)(2,1)}, bf16[8,32,256]{2,1,0:T(8,128)(2,1)S(1)}, u32[]{:S(2)}) %copy-start.2) | copy-done | bytes 131096
  56.2 0.0 copy-start.3
  56.2 0.6 %copy-done.3 = bf16[8,32,256]{2,1,0:T(8,128)(2,1)} copy-done((bf16[8,32,256]{2,1,0:T(8,128)(2,1)}, bf16[8,32,256]{2,1,0:T(8,128)(2,1)S(1)}, u32[]{:S(2)}) %copy-start.3) | copy-done | bytes 131096
  56.9 0.0 copy-start.6
  56.9 0.6 %copy-done.6 = f32[64,256]{1,0:T(8,128)} copy-done((f32[64,256]{1,0:T(8,128)}, f32[64,256]{1,0:T(8,128)S(1)}, u32[]{:S(2)}) %copy-start.6) | copy-done | bytes 65560
  57.5 0.0 copy-start.9
  57.5 0.6 copy-done.9
  58.1 1.7 %write_outputs.1 = (bf16[8,32,256]{2,1,0:T(8,128)(2,1)}, bf16[8,32,256]{2,1,0:T(8,128)(2,1)}, f32[7,7,256]{2,1,0:T(8,128)}, f32[1,256]{1,0:T(1,128)}, f32[2,256]...) custom-call(bf16[8,32,256]{2,1,0:T(8,128)(2,1)} %copy-done.2, ...), custom_call_target="tpu_custom_call" | custom-call | tf_op jit(solution)/shard_map/write_outputs/pallas_call | solution.py:469
Async XLA Ops:
  0.6 0.7 %copy-start.8 = (f32[1024]{0:T(1024)S(1)}, f32[1024]{0:T(1024)}, u32[]{:S(2)}) copy-start(f32[1024]{0:T(1024)} %param.12) | copy-start | bytes 12292
  0.6 0.7 %copy-start.10 = (f32[256]{0:T(256)S(1)}, f32[256]{0:T(256)}, u32[]{:S(2)}) copy-start(f32[256]{0:T(256)} %param.10) | copy-start | bytes 3076
  1.3 1.0 %copy-start = (bf16[256,1024]{1,0:T(8,128)(2,1)S(1)}, bf16[256,1024]{1,0:T(8,128)(2,1)}, u32[]{:S(2)}) copy-start(bf16[256,1024]{1,0:T(8,128)(2,1)} %w_in.1) | copy-start | bytes 1572868
  2.4 1.0 %copy-start.1 = (bf16[1024,256]{1,0:T(8,128)(2,1)S(1)}, bf16[1024,256]{1,0:T(8,128)(2,1)}, u32[]{:S(2)}) copy-start(bf16[1024,256]{1,0:T(8,128)(2,1)} %w_out.1) | copy-start | bytes 1572868
  3.4 0.9 %copy-start.4 = (bf16[8,32,256]{2,1,0:T(8,128)(2,1)S(1)}, bf16[8,32,256]{2,1,0:T(8,128)(2,1)}, u32[]{:S(2)}) copy-start(bf16[8,32,256]{2,1,0:T(8,128)(2,1)} %field.1) | copy-start | bytes 393220
  4.3 0.9 %copy-start.5 = (bf16[8,32,256]{2,1,0:T(8,128)(2,1)S(1)}, bf16[8,32,256]{2,1,0:T(8,128)(2,1)}, u32[]{:S(2)}) copy-start(bf16[8,32,256]{2,1,0:T(8,128)(2,1)} %cotangent.1) | copy-start | bytes 393220
  5.2 0.8 %copy-start.7 = (f32[7,7,256]{2,1,0:T(8,128)S(1)}, f32[7,7,256]{2,1,0:T(8,128)}, u32[]{:S(2)}) copy-start(f32[7,7,256]{2,1,0:T(8,128)} %taps.1) | copy-start | bytes 150532
  6.0 0.7 %copy-start.11 = (f32[256]{0:T(256)S(1)}, f32[256]{0:T(256)}, u32[]{:S(2)}) copy-start(f32[256]{0:T(256)} %param.14) | copy-start | bytes 3076
  55.6 0.7 %copy-start.2 = (bf16[8,32,256]{2,1,0:T(8,128)(2,1)}, bf16[8,32,256]{2,1,0:T(8,128)(2,1)S(1)}, u32[]{:S(2)}) copy-start(bf16[8,32,256]{2,1,0:T(8,128)(2,1)S(1)} %get-tuple-element.20.block_in) | copy-start | bytes 393220
  56.2 0.6 %copy-start.3 = (bf16[8,32,256]{2,1,0:T(8,128)(2,1)}, bf16[8,32,256]{2,1,0:T(8,128)(2,1)S(1)}, u32[]{:S(2)}) copy-start(bf16[8,32,256]{2,1,0:T(8,128)(2,1)S(1)} %get-tuple-element.21.field_in) | copy-start | bytes 393220
  56.9 0.6 %copy-start.6 = (f32[64,256]{1,0:T(8,128)}, f32[64,256]{1,0:T(8,128)S(1)}, u32[]{:S(2)}) copy-start(f32[64,256]{1,0:T(8,128)S(1)} %get-tuple-element.22.small) | copy-start | bytes 196612
  57.5 0.6 copy-start.9

commit v2 on v1

--- a/solution.py
+++ b/solution.py
@@ -21,6 +21,7 @@
 CHUNKS = 4
 CHUNK = FF // CHUNKS
 SUMS = 64
+VMEM_GRANT = 62 * 2**20
 FACTOR = 1.0 / 131072.0**0.5
 
 
@@ -50,8 +51,8 @@
     def sibling(self):
         return (self.lat + 1 - 2 * self.core, self.lon)
 
-    def on_x(self, x):
-        return (self.y_lo * 8 + x * 2 + self.core, self.lon)
+    def on_x(self, x, core=None):
+        return (self.y_lo * 8 + x * 2 + (self.core if core is None else core), self.lon)
 
     def on_y(self, y):
         return (lax.rem(y, 2) * 8 + self.x * 2 + self.core, (y // 2) * N_Z + self.z)
@@ -162,40 +163,68 @@
 
 
 def step(
-    field, taps, gain, w_in, b_in, w_out, layer_scale, cotangent,
-    block_out, grad_field, small_out, large_out,
-    pad, d_pad, conv, hat, normed, d_branch, inv_all, tmp,
+    field_hbm, taps_hbm, gain_hbm, w_in_hbm, b_in_hbm, w_out_hbm, layer_scale_hbm, cotangent_hbm,
+    block_hbm, grad_hbm, small_out, large_out,
+    block_out, grad_field, store,
+    field, taps, gain, w_in, b_in, w_out, layer_scale, cotangent, load,
+    pad, d_pad, conv, hat, normed, d_branch, inv_all, tmp, d_hidden, slope, branch,
     rows_out, cols_out, rows_in, cols_in, corners_in,
     d_rows_out, d_cols_out, d_rows_in, d_cols_in, d_corners_in,
-    part, part_in, x_out, x_in, y_out, y_in, z_out, z_in,
-    sums, sums_out, sums_in, sx, sy_a, sz_b, sz_a, sy_b, s_final,
+    part, part_in, x_out, x_in, y_out, y_in, z_out, z_in, zy_tmp, zy_out, zy_in, yz_out, yz_in,
+    sums, sums_out, sums_in, sx, sy_a, sz_b, sz_a, sy_b,
     halo_send, halo_recv, d_halo_send, d_halo_recv,
     core_send, core_recv, x_send, x_recv, y_send, y_recv, z_send, z_recv,
-    s_core_send, s_core_recv, sx_send, sx_recv, s3_send, s3_recv, s4_send, s4_recv, s_all_send, s_all_recv,
+    zy_send, zy_recv, yz_send, yz_recv,
+    s_core_send, s_core_recv, sx_send, sx_recv, s3_send, s3_recv, s4_send, s4_recv,
 ):
+    loads = [
+        pltpu.make_async_copy(src, dst, load.at[at])
+        for at, (src, dst) in enumerate((
+            (field_hbm, field),
+            (cotangent_hbm, cotangent),
+            (layer_scale_hbm, layer_scale),
+            (taps_hbm, taps),
+            (gain_hbm, gain),
+            (w_in_hbm, w_in),
+            (b_in_hbm, b_in),
+            (w_out_hbm, w_out),
+        ))
+    ]
+    for copy in loads:
+        copy.start()
+
     place = Place()
     core, x, y, z = place.core, place.x, place.y, place.z
 
     barrier = pltpu.get_barrier_semaphore()
     partners = [place.grid(*side) for side in SIDES]
     partners.append(place.sibling())
-    partners += [place.on_x(lax.rem(x + k, N_X)) for k in range(1, N_X)]
+    partners += [place.on_x(lax.rem(x + k, N_X), c) for k in range(1, N_X) for c in range(2)]
     partners += [place.on_y(lax.rem(y + k, N_Y)) for k in range(1, N_Y)]
     partners += [place.on_z(lax.rem(z + k, N_Z)) for k in range(1, N_Z)]
     for device in partners:
         pl.semaphore_signal(barrier, inc=1, device_id=device, device_id_type=MESH)
 
+    loads[0].wait()
     for half in range(2):
         lanes = slice(half * HALF, (half + 1) * HALF)
         pad[half, 3 : 3 + ROWS, LEFT : LEFT + COLS, :] = field[:, :, lanes].astype(F32)
     halo_pack(pad, tmp, rows_out, cols_out)
-    wide_cot = cotangent[...].reshape(CELLS, CH).astype(F32)
-    d_branch[...] = (layer_scale[...] * wide_cot).astype(BF16)
-
     pl.semaphore_wait(barrier, len(partners))
     halos = halo_copies(place, rows_out, cols_out, rows_in, cols_in, corners_in, halo_send, halo_recv)
     for copy in halos:
         copy.start()
+
+    for copy in loads[1:]:
+        copy.wait()
+    wide_cot = cotangent[...].reshape(CELLS, CH).astype(F32)
+    d_branch[...] = (layer_scale[...] * wide_cot).astype(BF16)
+    for chunk in range(CHUNKS):
+        d_hidden[chunk] = dot(d_branch[...], w_out[chunk * CHUNK : (chunk + 1) * CHUNK, :], 1, 1)
+    z_out[...] = jnp.zeros_like(z_out)
+    yz_out[...] = jnp.zeros_like(yz_out)
+    sums[55:64, :] = jnp.zeros((9, CH), F32)
+
     for copy in halos:
         copy.wait()
     halo_unpack(place, pad, rows_in, cols_in, corners_in)
@@ -213,35 +242,61 @@
         hat[half] = value
         normed[:, lanes] = (value * gain[:, lanes]).astype(BF16)
 
-    branch = jnp.zeros((CELLS, CH), F32)
-    d_normed = jnp.zeros((CELLS, CH), F32)
-    core_copies = []
+    core_copies = {}
+    x_copies = {}
+
+    def send_on_core(which, chunk, value):
+        part[which, chunk] = value.astype(BF16).reshape(2, 2, 64, CH)
+        copy = remote(
+            part.at[which, chunk, :, 1 - core], part_in.at[which, chunk],
+            core_send.at[which, chunk], core_recv.at[which, chunk], place.sibling(),
+        )
+        copy.start()
+        core_copies[which, chunk] = copy
+
+    def send_on_x(which, chunk):
+        core_copies[which, chunk].wait()
+        both = part[which, chunk, :, core].astype(F32) + part_in[which, chunk].astype(F32)
+        row = chunk // 2
+        x_out[which, row, (chunk % 2) * 2 : (chunk % 2) * 2 + 2] = both.astype(BF16)
+        if chunk % 2 == 1:
+            for k in range(1, N_X):
+                to = lax.rem(x + k, N_X)
+                copy = remote(
+                    x_out.at[which, row, to], x_in.at[which, k - 1, row],
+                    x_send.at[which, k - 1, row], x_recv.at[which, k - 1, row], place.on_x(to),
+                )
+                copy.start()
+                x_copies[which, k, row] = copy
+
+    total = jnp.zeros((CELLS, CH), F32)
     for chunk in range(CHUNKS):
         hidden_units = slice(chunk * CHUNK, (chunk + 1) * CHUNK)
         pre_act = dot(normed[...], w_in[:, hidden_units], 1, 0) + b_in[:, hidden_units]
         value, gelu_slope = gelu_pair(pre_act)
         hidden = value.astype(BF16)
-        d_pre = dot(d_branch[...], w_out[hidden_units, :], 1, 1) * gelu_slope
+        slope[chunk] = gelu_slope
+        send_on_core(1, chunk, dot(hidden, d_branch[...], 0, 0))
+        total = total + dot(hidden, w_out[hidden_units, :], 1, 0)
+        if chunk >= 2:
+            send_on_x(1, chunk - 2)
+    branch[...] = total
+
+    d_normed = jnp.zeros((CELLS, CH), F32)
+    for chunk in range(CHUNKS):
+        hidden_units = slice(chunk * CHUNK, (chunk + 1) * CHUNK)
+        d_pre = d_hidden[chunk] * slope[chunk]
         d_pre_b = d_pre.astype(BF16)
-        part[1, chunk] = dot(hidden, d_branch[...], 0, 0).astype(BF16).reshape(2, 2, 64, CH)
-        part[0, chunk] = dot(d_pre_b, normed[...], 0, 0).astype(BF16).reshape(2, 2, 64, CH)
-        for which in (1, 0):
-            copy = remote(
-                part.at[which, chunk, :, 1 - core], part_in.at[which, chunk],
-                core_send.at[which, chunk], core_recv.at[which, chunk], place.sibling(),
-            )
-            copy.start()
-            core_copies.append((which, chunk, copy))
-        branch = branch + dot(hidden, w_out[hidden_units, :], 1, 0)
+        send_on_core(0, chunk, dot(d_pre_b, normed[...], 0, 0))
         d_normed = d_normed + dot(d_pre_b, w_in[:, hidden_units], 1, 1)
         sums[51 + chunk : 52 + chunk, :] = jnp.sum(d_pre, axis=0, keepdims=True)
+        if chunk < 2:
+            send_on_x(1, chunk + 2)
+        else:
+            send_on_x(0, chunk - 2)
 
     wide_cot = cotangent[...].reshape(CELLS, CH).astype(F32)
-    sums[50:51, :] = jnp.sum(wide_cot * branch, axis=0, keepdims=True)
-    sums[55:64, :] = jnp.zeros((9, CH), F32)
-    block_out[...] = (
-        field[...].reshape(CELLS, CH).astype(F32) + layer_scale[...] * branch
-    ).astype(BF16).reshape(ROWS, COLS, CH)
+    sums[50:51, :] = jnp.sum(wide_cot * branch[...], axis=0, keepdims=True)
 
     hats = [hat[half] for half in range(2)]
     d_halves = [d_normed[:, half * HALF : (half + 1) * HALF] for half in range(2)]
@@ -263,51 +318,20 @@
     for copy in d_halos:
         copy.start()
 
-    x_copies = []
-    for which, chunk, copy in core_copies:
-        copy.wait()
-        both = part[which, chunk, :, core].astype(F32) + part_in[which, chunk].astype(F32)
-        x_out[which, chunk // 2, (chunk % 2) * 2 : (chunk % 2) * 2 + 2] = both.astype(BF16)
-    for which in (1, 0):
-        for k in range(1, N_X):
-            to = lax.rem(x + k, N_X)
-            copy = remote(
-                x_out.at[which, :, to], x_in.at[which, k - 1],
-                x_send.at[which, k - 1], x_recv.at[which, k - 1], place.on_x(to),
-            )
-            copy.start()
-            x_copies.append(copy)
+    send_on_x(0, 2)
+    send_on_x(0, 3)
 
     tap_sums(pad, d_pad, sums)
 
-    sums_out[...] = sums[...].reshape(2, SUMS // 2, CH).astype(BF16)
-    s_core = remote(sums_out.at[1 - core], sums_in, s_core_send, s_core_recv, place.sibling())
-    s_core.start()
-
-    y_copies = []
-    for which in (1, 0):
-        total = x_out[which, :, x].astype(F32)
-        for k in range(1, N_X):
-            x_copies[(1 - which) * (N_X - 1) + k - 1].wait()
-            total = total + x_in[which, k - 1].astype(F32)
-        y_out[which] = total.astype(BF16).reshape(2, 4, 16, CH)
-        if which == 1:
-            s_core.wait()
-            sx[x] = (sums_out[core].astype(F32) + sums_in[...].astype(F32)).astype(BF16)
-            sx_copies = []
-            for k in range(1, N_X):
-                to = lax.rem(x + k, N_X)
-                copy = remote(sx.at[x], sx.at[x], sx_send.at[to], sx_recv.at[x], place.on_x(to))
-                copy.start()
-                sx_copies.append(copy)
-        for k in range(1, N_Y):
-            to = lax.rem(y + k, N_Y)
-            copy = remote(
-                y_out.at[which, lax.rem(to, 2), to // 2], y_in.at[which, k - 1],
-                y_send.at[which, k - 1], y_recv.at[which, k - 1], place.on_y(to),
-            )
-            copy.start()
-            y_copies.append(copy)
+    def wait_slots(slots, send, recv, own, count, device_on):
+        for k in range(1, count):
+            other = lax.rem(own + k, count)
+            remote(slots.at[own], slots.at[other], send.at[other], recv.at[other], device_on(other)).wait()
+
+    def share(slots, send, recv, own, count, device_on):
+        for k in range(1, count):
+            other = lax.rem(own + k, count)
+            remote(slots.at[own], slots.at[own], send.at[other], recv.at[own], device_on(other)).start()
 
     def gather_sum(slots, count):
         total = slots[0].astype(F32)
@@ -315,23 +339,21 @@
             total = total + slots[at].astype(F32)
         return total
 
-    def wait_slots(slots, send, recv, own, count, device_on):
-        for k in range(1, count):
-            other = lax.rem(own + k, count)
-            remote(slots.at[own], slots.at[other], send.at[other], recv.at[other], device_on(other)).wait()
-
-    def share(slots, send, recv, own, count, device_on):
-        for k in range(1, count):
-            other = lax.rem(own + k, count)
-            remote(slots.at[own], slots.at[own], send.at[other], recv.at[own], device_on(other)).start()
-
-    wait_slots(sx, sx_send, sx_recv, x, N_X, place.on_x)
-    total = gather_sum(sx, N_X).astype(BF16)
+    sums_out[...] = sums[...].reshape(2, SUMS // 2, CH).astype(BF16)
+    s_core = remote(sums_out.at[1 - core], sums_in, s_core_send, s_core_recv, place.sibling())
+    s_core.start()
+    s_core.wait()
+    total = (sums_out[core].astype(F32) + sums_in[...].astype(F32)).astype(BF16)
     sy_a[y] = total[0:16]
     sz_b[z] = total[16:32]
     share(sy_a, s3_send.at[0], s3_recv.at[0], y, N_Y, place.on_y)
     share(sz_b, s3_send.at[1], s3_recv.at[1], z, N_Z, place.on_z)
 
+    block_out[...] = (
+        field[...].reshape(CELLS, CH).astype(F32) + layer_scale[...] * branch[...]
+    ).astype(BF16).reshape(ROWS, COLS, CH)
+    block_store = pltpu.make_async_copy(block_out, block_hbm, store.at[0])
+    block_store.start()
     for copy in d_halos:
         copy.wait()
     halo_unpack(place, d_pad, d_rows_in, d_cols_in, d_corners_in)
@@ -339,53 +361,106 @@
     for half in range(2):
         lanes = slice(half * HALF, (half + 1) * HALF)
         grad_field[:, :, lanes] = (cotangent[:, :, lanes].astype(F32) + conv[half]).astype(BF16)
-
-    for which in (1, 0):
-        total = y_out[which, place.y_lo, place.y_hi].astype(F32)
-        for k in range(1, N_Y):
-            y_copies[(1 - which) * (N_Y - 1) + k - 1].wait()
-            total = total + y_in[which, k - 1].astype(F32)
-        for to in range(N_Z):
-            for half in range(2):
-                at = which * 4 + half * 2
-                z_out[to, at : at + 2, :] = total[2 * to : 2 * to + 2, half * HALF : (half + 1) * HALF]
-    z_copies = []
-    for k in range(1, N_Z):
-        to = lax.rem(z + k, N_Z)
-        copy = remote(z_out.at[to], z_in.at[k - 1], z_send.at[k - 1], z_recv.at[k - 1], place.on_z(to))
-        copy.start()
-        z_copies.append(copy)
+    grad_store = pltpu.make_async_copy(grad_field, grad_hbm, store.at[1])
+    grad_store.start()
 
     wait_slots(sy_a, s3_send.at[0], s3_recv.at[0], y, N_Y, place.on_y)
+    sz_a[z] = gather_sum(sy_a, N_Y).astype(BF16)
+    share(sz_a, s4_send.at[0], s4_recv.at[0], z, N_Z, place.on_z)
     wait_slots(sz_b, s3_send.at[1], s3_recv.at[1], z, N_Z, place.on_z)
-    sz_a[z] = gather_sum(sy_a, N_Y).astype(BF16)
     sy_b[y] = gather_sum(sz_b, N_Z).astype(BF16)
-    share(sz_a, s4_send.at[0], s4_recv.at[0], z, N_Z, place.on_z)
     share(sy_b, s4_send.at[1], s4_recv.at[1], y, N_Y, place.on_y)
 
-    total = z_out[z]
-    for k in range(1, N_Z):
-        z_copies[k - 1].wait()
-        total = total + z_in[k - 1]
-    large_out[...] = total * FACTOR
+    def sum_on_x(which):
+        for k in range(1, N_X):
+            for row in range(2):
+                x_copies[which, k, row].wait()
+        total = x_out[which, :, x].astype(F32)
+        for k in range(1, N_X):
+            total = total + x_in[which, k - 1].astype(F32)
+        return total
+
+    def spread(into, send, recv, own, count, device_on, block):
+        copies = []
+        for k in range(1, count):
+            to = lax.rem(own + k, count)
+            copy = remote(block(to), into.at[k - 1], send.at[k - 1], recv.at[k - 1], device_on(to))
+            copy.start()
+            copies.append(copy)
+        return copies
+
+    def collect(copies, total, into):
+        for copy in copies:
+            copy.wait()
+        for at in range(len(copies)):
+            total = total + into[at].astype(F32)
+        return total
+
+    y_out[...] = sum_on_x(1).astype(BF16).reshape(2, 4, 16, CH)
+    y_copies = spread(
+        y_in, y_send, y_recv, y, N_Y, place.on_y,
+        lambda to: y_out.at[lax.rem(to, 2), to // 2],
+    )
+    total = sum_on_x(0).reshape(2, 4, 16, CH)
+    for on_y in range(N_Y):
+        for on_z in range(N_Z):
+            zy_tmp[on_z, 2 * on_y : 2 * on_y + 2, :] = total[on_y % 2, on_y // 2, 2 * on_z : 2 * on_z + 2]
+    zy_out[...] = zy_tmp[...].astype(BF16)
+    zy_copies = spread(
+        zy_in, zy_send, zy_recv, z, N_Z, place.on_z, lambda to: zy_out.at[to]
+    )
 
     wait_slots(sz_a, s4_send.at[0], s4_recv.at[0], z, N_Z, place.on_z)
     wait_slots(sy_b, s4_send.at[1], s4_recv.at[1], y, N_Y, place.on_y)
-    s_final[core, 0:16] = gather_sum(sz_a, N_Z) * FACTOR
-    s_final[core, 16:32] = gather_sum(sy_b, N_Y) * FACTOR
-    s_all = remote(s_final.at[core], s_final.at[core], s_all_send, s_all_recv, place.sibling())
-    s_all.start()
-    s_all.wait_send()
-    remote(s_final.at[core], s_final.at[1 - core], s_all_send, s_all_recv, place.sibling()).wait_recv()
-    small_out[...] = s_final[...].reshape(SUMS, CH)
+    sx[core, x, 0:16] = gather_sum(sz_a, N_Z).astype(BF16)
+    sx[core, x, 16:32] = gather_sum(sy_b, N_Y).astype(BF16)
+    last = [(c, k) for c in range(2) for k in range(N_X) if (c, k) != (0, 0)]
+    for c, k in last:
+        c, k = lax.rem(core + c, 2), lax.rem(x + k, N_X)
+        remote(
+            sx.at[core, x], sx.at[core, x], sx_send.at[c, k], sx_recv.at[core, x], place.on_x(k, c)
+        ).start()
+
+    def pack(out, first, total):
+        for to in range(8):
+            for half in range(2):
+                at = first + half * 2
+                out[to, at : at + 2, :] = total[2 * to : 2 * to + 2, half * HALF : (half + 1) * HALF]
+
+    pack(z_out, 4, collect(y_copies, y_out[place.y_lo, place.y_hi].astype(F32), y_in))
+    z_copies = spread(z_in, z_send, z_recv, z, N_Z, place.on_z, lambda to: z_out.at[to])
+    pack(yz_out, 0, collect(zy_copies, zy_out[z].astype(F32), zy_in))
+    yz_copies = spread(yz_in, yz_send, yz_recv, y, N_Y, place.on_y, lambda to: yz_out.at[to])
+
+    for c, k in last:
+        c, k = lax.rem(core + c, 2), lax.rem(x + k, N_X)
+        remote(
+            sx.at[core, x], sx.at[c, k], sx_send.at[c, k], sx_recv.at[c, k], place.on_x(k, c)
+        ).wait()
+    for c in range(2):
+        small_out[c * (SUMS // 2) : (c + 1) * (SUMS // 2), :] = gather_sum(sx.at[c], N_X) * FACTOR
+
+    large_out[4:8, :] = collect(z_copies, z_out[z], z_in)[4:8] * FACTOR
+    large_out[0:4, :] = collect(yz_copies, yz_out[y], yz_in)[0:4] * FACTOR
+    block_store.wait()
+    grad_store.wait()
 
 
 def finish(
-    block_in, field_in, small, large,
+    block_in, grad_in_hbm, small_hbm, large_hbm,
     block_out, grad_field, grad_taps, grad_gain, grad_in, grad_bias, grad_out, grad_scale,
+    small, large, move,
 ):
-    block_out[...] = block_in[...]
-    grad_field[...] = field_in[...]
+    moves = [
+        pltpu.make_async_copy(src, dst, move.at[at])
+        for at, (src, dst) in enumerate((
+            (small_hbm, small), (large_hbm, large), (block_in, block_out), (grad_in_hbm, grad_field),
+        ))
+    ]
+    for copy in moves:
+        copy.start()
+    moves[0].wait()
+    moves[1].wait()
     for a in range(7):
         grad_taps[a] = small[a * 7 : a * 7 + 7, :]
     grad_gain[...] = small[49:50, :]
@@ -396,6 +471,8 @@
         lanes = slice(half * HALF, (half + 1) * HALF)
         grad_in[:, lanes] = large[half * 2 : half * 2 + 2, :]
         grad_out[:, lanes] = large[4 + half * 2 : 6 + half * 2, :]
+    moves[2].wait()
+    moves[3].wait()
 
 
 def local(field, kernel, gain, w_in, b_in, w_out, layer_scale, cotangent):
@@ -408,7 +485,20 @@
         pltpu.VMEM((2, 4 * ROWS, CH), BF16),
         pltpu.VMEM((4, 16, CH), BF16),
     ]
+    hbm = pl.BlockSpec(memory_space=pltpu.HBM)
     scratch = [
+        pltpu.VMEM((ROWS, COLS, CH), BF16),
+        pltpu.VMEM((ROWS, COLS, CH), BF16),
+        dma((2,)),
+        pltpu.VMEM((ROWS, COLS, CH), BF16),
+        pltpu.VMEM((7, 7, CH), F32),
+        pltpu.VMEM((1, CH), F32),
+        pltpu.VMEM((CH, FF), BF16),
+        pltpu.VMEM((1, FF), F32),
+        pltpu.VMEM((FF, CH), BF16),
+        pltpu.VMEM((1, CH), F32),
+        pltpu.VMEM((ROWS, COLS, CH), BF16),
+        dma((8,)),
         pltpu.VMEM((2, ROWS + 6, COLS + 16, HALF), F32),
         pltpu.VMEM((2, ROWS + 6, COLS + 16, HALF), F32),
         pltpu.VMEM((2, ROWS, COLS, HALF), F32),
@@ -417,34 +507,40 @@
         pltpu.VMEM((CELLS, CH), BF16),
         pltpu.VMEM((CELLS, HALF), F32),
         pltpu.VMEM((2, 4 * ROWS, CH), F32),
+        pltpu.VMEM((CHUNKS, CELLS, CHUNK), F32),
+        pltpu.VMEM((CHUNKS, CELLS, CHUNK), F32),
+        pltpu.VMEM((CELLS, CH), F32),
         *halo,
         *halo,
         pltpu.VMEM((2, CHUNKS, 2, 2, 64, CH), BF16),
         pltpu.VMEM((2, CHUNKS, 2, 64, CH), BF16),
         pltpu.VMEM((2, 2, N_X, 64, CH), BF16),
         pltpu.VMEM((2, N_X - 1, 2, 64, CH), BF16),
-        pltpu.VMEM((2, 2, 4, 16, CH), BF16),
-        pltpu.VMEM((2, N_Y - 1, 16, CH), BF16),
+        pltpu.VMEM((2, 4, 16, CH), BF16),
+        pltpu.VMEM((N_Y - 1, 16, CH), BF16),
         pltpu.VMEM((N_Z, 8, HALF), F32),
         pltpu.VMEM((N_Z - 1, 8, HALF), F32),
+        pltpu.VMEM((N_Z, 16, CH), F32),
+        pltpu.VMEM((N_Z, 16, CH), BF16),
+        pltpu.VMEM((N_Z - 1, 16, CH), BF16),
+        pltpu.VMEM((N_Y, 8, HALF), F32),
+        pltpu.VMEM((N_Y - 1, 8, HALF), F32),
         pltpu.VMEM((SUMS, CH), F32),
         pltpu.VMEM((2, SUMS // 2, CH), BF16),
         pltpu.VMEM((SUMS // 2, CH), BF16),
-        pltpu.VMEM((N_X, SUMS // 2, CH), BF16),
+        pltpu.VMEM((2, N_X, SUMS // 2, CH), BF16),
         pltpu.VMEM((N_Y, 16, CH), BF16),
         pltpu.VMEM((N_Z, 16, CH), BF16),
         pltpu.VMEM((N_Z, 16, CH), BF16),
         pltpu.VMEM((N_Y, 16, CH), BF16),
-        pltpu.VMEM((2, SUMS // 2, CH), F32),
         dma((8,)), dma((8,)), dma((8,)), dma((8,)),
         dma((2, CHUNKS)), dma((2, CHUNKS)),
-        dma((2, N_X - 1)), dma((2, N_X - 1)),
-        dma((2, N_Y - 1)), dma((2, N_Y - 1)),
-        dma((N_Z - 1,)), dma((N_Z - 1,)),
+        dma((2, N_X - 1, 2)), dma((2, N_X - 1, 2)),
+        dma((N_Y - 1,)), dma((N_Y - 1,)), dma((N_Z - 1,)), dma((N_Z - 1,)),
+        dma((N_Z - 1,)), dma((N_Z - 1,)), dma((N_Y - 1,)), dma((N_Y - 1,)),
         dma, dma,
-        dma((N_X,)), dma((N_X,)),
+        dma((2, N_X)), dma((2, N_X)),
         dma((2, 8)), dma((2, 8)), dma((2, 8)), dma((2, 8)),
-        dma, dma,
     ]
     grid_shape = jax.ShapeDtypeStruct(field.shape, BF16)
     mids = pl.pallas_call(
@@ -455,11 +551,11 @@
             jax.ShapeDtypeStruct((SUMS, CH), F32),
             jax.ShapeDtypeStruct((8, HALF), F32),
         ),
-        in_specs=[vmem] * 8,
-        out_specs=[vmem] * 4,
+        in_specs=[hbm] * 8,
+        out_specs=[hbm, hbm, vmem, vmem],
         scratch_shapes=scratch,
         compiler_params=pltpu.CompilerParams(
-            collective_id=0, has_side_effects=True, vmem_limit_bytes=48 * 2**20
+            collective_id=0, has_side_effects=True, vmem_limit_bytes=VMEM_GRANT
         ),
         name="block_step",
     )(
@@ -478,8 +574,10 @@
             jax.ShapeDtypeStruct((2, CH), F32),
             jax.ShapeDtypeStruct((1, CH), F32),
         ),
-        in_specs=[vmem] * 4,
+        in_specs=[hbm] * 4,
         out_specs=[vmem] * 8,
+        scratch_shapes=[pltpu.VMEM((SUMS, CH), F32), pltpu.VMEM((8, HALF), F32), dma((4,))],
+        compiler_params=pltpu.CompilerParams(vmem_limit_bytes=VMEM_GRANT),
         name="write_outputs",
     )(*mids)
     return (

time: 60.2 us -> 50.8 us (0.84)
  the two profiles are of different devices: /device:TPU:1 before, /device:TPU:8 now
where the time goes in v2:
time: 50.8 us; the launch traced here: 50.7 us
  Pallas kernels  50 us (98%)
  between operations  0.64 us (1%)
    pallas_call x1, Pallas kernels, local(): pl.pallas_call(step, out_shape=(grid_shape, grid_shape, jax.ShapeDtypeStr...  48.2 us
    pallas_call x1, Pallas kernels, local(): pl.pallas_call(finish, out_shape=(grid_shape, grid_shape, jax.ShapeDtypeS...  1.77 us

profile of v2, /device:TPU:8, one launch (start us, length us, event | category | flops | bytes accessed | tf_op | source)
XLA Modules:
  0.0 50.7 jit_solution(3310874300732298993)
XLA Ops:
  0.6 48.2 %block_step.1 = (bf16[8,32,256]{2,1,0:T(8,128)(2,1)}, bf16[8,32,256]{2,1,0:T(8,128)(2,1)}, f32[64,256]{1,0:T(8,128)}, f32[8,128]{1,0:T(8,128)}) custom-call(bf16[8,32,256]{2,1,0:T(8,128)(2,1)} %field_hbm.1, f32[7,7,256]{2,1,0:T(8,128)} %taps_hbm.1, f32[1,256]{1,0:T(1,128)} %bitcast.8, bf16[256,1024]{1,0:T(8,128)(2,1)} %w_in_hbm.1, f32[1,1024]{1,0:T(1,128)} %bitcast.7, ...), custom_call_target="tpu_custom_call" | custom-call | tf_op jit(solution)/shard_map/block_step/pallas_call | solution.py:546
  48.9 1.8 %write_outputs.1 = (bf16[8,32,256]{2,1,0:T(8,128)(2,1)}, bf16[8,32,256]{2,1,0:T(8,128)(2,1)}, f32[7,7,256]{2,1,0:T(8,128)}, f32[1,256]{1,0:T(1,128)}, f32[2,256]...) custom-call(bf16[8,32,256]{2,1,0:T(8,128)(2,1)} %get-tuple-element.20.block_in, ...), custom_call_target="tpu_custom_call" | custom-call | tf_op jit(solution)/shard_map/write_outputs/pallas_call | solution.py:565

commit v3 on v2

--- a/solution.py
+++ b/solution.py
@@ -190,20 +190,20 @@
             (w_out_hbm, w_out),
         ))
     ]
-    for copy in loads:
-        copy.start()
 
     place = Place()
     core, x, y, z = place.core, place.x, place.y, place.z
 
     barrier = pltpu.get_barrier_semaphore()
-    partners = [place.grid(*side) for side in SIDES]
-    partners.append(place.sibling())
+    partners = [place.grid(*side) for side in SIDES[::-1]]
     partners += [place.on_x(lax.rem(x + k, N_X), c) for k in range(1, N_X) for c in range(2)]
     partners += [place.on_y(lax.rem(y + k, N_Y)) for k in range(1, N_Y)]
     partners += [place.on_z(lax.rem(z + k, N_Z)) for k in range(1, N_Z)]
+    partners.append(place.sibling())
     for device in partners:
         pl.semaphore_signal(barrier, inc=1, device_id=device, device_id_type=MESH)
+    for copy in loads:
+        copy.start()
 
     loads[0].wait()
     for half in range(2):
@@ -212,7 +212,7 @@
     halo_pack(pad, tmp, rows_out, cols_out)
     pl.semaphore_wait(barrier, len(partners))
     halos = halo_copies(place, rows_out, cols_out, rows_in, cols_in, corners_in, halo_send, halo_recv)
-    for copy in halos:
+    for copy in halos[::-1]:
         copy.start()
 
     for copy in loads[1:]:
@@ -242,32 +242,28 @@
         hat[half] = value
         normed[:, lanes] = (value * gain[:, lanes]).astype(BF16)
 
-    core_copies = {}
-    x_copies = {}
-
-    def send_on_core(which, chunk, value):
-        part[which, chunk] = value.astype(BF16).reshape(2, 2, 64, CH)
+    def send_on_core(which):
         copy = remote(
-            part.at[which, chunk, :, 1 - core], part_in.at[which, chunk],
-            core_send.at[which, chunk], core_recv.at[which, chunk], place.sibling(),
+            part.at[which, :, :, 1 - core], part_in.at[which],
+            core_send.at[which], core_recv.at[which], place.sibling(),
         )
         copy.start()
-        core_copies[which, chunk] = copy
-
-    def send_on_x(which, chunk):
-        core_copies[which, chunk].wait()
-        both = part[which, chunk, :, core].astype(F32) + part_in[which, chunk].astype(F32)
-        row = chunk // 2
-        x_out[which, row, (chunk % 2) * 2 : (chunk % 2) * 2 + 2] = both.astype(BF16)
-        if chunk % 2 == 1:
-            for k in range(1, N_X):
-                to = lax.rem(x + k, N_X)
-                copy = remote(
-                    x_out.at[which, row, to], x_in.at[which, k - 1, row],
-                    x_send.at[which, k - 1, row], x_recv.at[which, k - 1, row], place.on_x(to),
-                )
-                copy.start()
-                x_copies[which, k, row] = copy
+        return copy
+
+    def send_on_x(which, core_copy):
+        core_copy.wait()
+        both = part[which, :, :, core].astype(F32) + part_in[which].astype(F32)
+        x_out[which] = both.astype(BF16).reshape(2, N_X, 64, CH)
+        copies = []
+        for k in range(1, N_X):
+            to = lax.rem(x + k, N_X)
+            copy = remote(
+                x_out.at[which, :, to], x_in.at[which, k - 1],
+                x_send.at[which, k - 1], x_recv.at[which, k - 1], place.on_x(to),
+            )
+            copy.start()
+            copies.append(copy)
+        return copies
 
     total = jnp.zeros((CELLS, CH), F32)
     for chunk in range(CHUNKS):
@@ -276,24 +272,20 @@
         value, gelu_slope = gelu_pair(pre_act)
         hidden = value.astype(BF16)
         slope[chunk] = gelu_slope
-        send_on_core(1, chunk, dot(hidden, d_branch[...], 0, 0))
+        part[1, chunk] = dot(hidden, d_branch[...], 0, 0).astype(BF16).reshape(2, 2, 64, CH)
         total = total + dot(hidden, w_out[hidden_units, :], 1, 0)
-        if chunk >= 2:
-            send_on_x(1, chunk - 2)
     branch[...] = total
+    core_out = send_on_core(1)
 
     d_normed = jnp.zeros((CELLS, CH), F32)
     for chunk in range(CHUNKS):
         hidden_units = slice(chunk * CHUNK, (chunk + 1) * CHUNK)
         d_pre = d_hidden[chunk] * slope[chunk]
         d_pre_b = d_pre.astype(BF16)
-        send_on_core(0, chunk, dot(d_pre_b, normed[...], 0, 0))
+        part[0, chunk] = dot(d_pre_b, normed[...], 0, 0).astype(BF16).reshape(2, 2, 64, CH)
         d_normed = d_normed + dot(d_pre_b, w_in[:, hidden_units], 1, 1)
         sums[51 + chunk : 52 + chunk, :] = jnp.sum(d_pre, axis=0, keepdims=True)
-        if chunk < 2:
-            send_on_x(1, chunk + 2)
-        else:
-            send_on_x(0, chunk - 2)
+    core_in = send_on_core(0)
 
     wide_cot = cotangent[...].reshape(CELLS, CH).astype(F32)
     sums[50:51, :] = jnp.sum(wide_cot * branch[...], axis=0, keepdims=True)
@@ -311,15 +303,8 @@
         d_conv = inv_all[...] * (scaled[half] - m1 - hats[half] * m2)
         d_pad[half, 3 : 3 + ROWS, LEFT : LEFT + COLS, :] = d_conv.reshape(ROWS, COLS, HALF)
 
-    halo_pack(d_pad, tmp, d_rows_out, d_cols_out)
-    d_halos = halo_copies(
-        place, d_rows_out, d_cols_out, d_rows_in, d_cols_in, d_corners_in, d_halo_send, d_halo_recv
-    )
-    for copy in d_halos:
-        copy.start()
-
-    send_on_x(0, 2)
-    send_on_x(0, 3)
+
+    x_copies_out = send_on_x(1, core_out)
 
     tap_sums(pad, d_pad, sums)
 
@@ -342,6 +327,14 @@
     sums_out[...] = sums[...].reshape(2, SUMS // 2, CH).astype(BF16)
     s_core = remote(sums_out.at[1 - core], sums_in, s_core_send, s_core_recv, place.sibling())
     s_core.start()
+    halo_pack(d_pad, tmp, d_rows_out, d_cols_out)
+    d_halos = halo_copies(
+        place, d_rows_out, d_cols_out, d_rows_in, d_cols_in, d_corners_in, d_halo_send, d_halo_recv
+    )
+    for copy in d_halos:
+        copy.start()
+
+    x_copies_in = send_on_x(0, core_in)
     s_core.wait()
     total = (sums_out[core].astype(F32) + sums_in[...].astype(F32)).astype(BF16)
     sy_a[y] = total[0:16]
@@ -354,27 +347,10 @@
     ).astype(BF16).reshape(ROWS, COLS, CH)
     block_store = pltpu.make_async_copy(block_out, block_hbm, store.at[0])
     block_store.start()
-    for copy in d_halos:
-        copy.wait()
-    halo_unpack(place, d_pad, d_rows_in, d_cols_in, d_corners_in)
-    depthwise(d_pad, taps, conv, True)
-    for half in range(2):
-        lanes = slice(half * HALF, (half + 1) * HALF)
-        grad_field[:, :, lanes] = (cotangent[:, :, lanes].astype(F32) + conv[half]).astype(BF16)
-    grad_store = pltpu.make_async_copy(grad_field, grad_hbm, store.at[1])
-    grad_store.start()
-
-    wait_slots(sy_a, s3_send.at[0], s3_recv.at[0], y, N_Y, place.on_y)
-    sz_a[z] = gather_sum(sy_a, N_Y).astype(BF16)
-    share(sz_a, s4_send.at[0], s4_recv.at[0], z, N_Z, place.on_z)
-    wait_slots(sz_b, s3_send.at[1], s3_recv.at[1], z, N_Z, place.on_z)
-    sy_b[y] = gather_sum(sz_b, N_Z).astype(BF16)
-    share(sy_b, s4_send.at[1], s4_recv.at[1], y, N_Y, place.on_y)
-
-    def sum_on_x(which):
-        for k in range(1, N_X):
-            for row in range(2):
-                x_copies[which, k, row].wait()
+
+    def sum_on_x(which, copies):
+        for copy in copies:
+            copy.wait()
         total = x_out[which, :, x].astype(F32)
         for k in range(1, N_X):
             total = total + x_in[which, k - 1].astype(F32)
@@ -396,12 +372,12 @@
             total = total + into[at].astype(F32)
         return total
 
-    y_out[...] = sum_on_x(1).astype(BF16).reshape(2, 4, 16, CH)
+    y_out[...] = sum_on_x(1, x_copies_out).astype(BF16).reshape(2, 4, 16, CH)
     y_copies = spread(
         y_in, y_send, y_recv, y, N_Y, place.on_y,
         lambda to: y_out.at[lax.rem(to, 2), to // 2],
     )
-    total = sum_on_x(0).reshape(2, 4, 16, CH)
+    total = sum_on_x(0, x_copies_in).reshape(2, 4, 16, CH)
     for on_y in range(N_Y):
         for on_z in range(N_Z):
             zy_tmp[on_z, 2 * on_y : 2 * on_y + 2, :] = total[on_y % 2, on_y // 2, 2 * on_z : 2 * on_z + 2]
@@ -409,6 +385,32 @@
     zy_copies = spread(
         zy_in, zy_send, zy_recv, z, N_Z, place.on_z, lambda to: zy_out.at[to]
     )
+
+    wait_slots(sy_a, s3_send.at[0], s3_recv.at[0], y, N_Y, place.on_y)
+    sz_a[z] = gather_sum(sy_a, N_Y).astype(BF16)
+    share(sz_a, s4_send.at[0], s4_recv.at[0], z, N_Z, place.on_z)
+    wait_slots(sz_b, s3_send.at[1], s3_recv.at[1], z, N_Z, place.on_z)
+    sy_b[y] = gather_sum(sz_b, N_Z).astype(BF16)
+    share(sy_b, s4_send.at[1], s4_recv.at[1], y, N_Y, place.on_y)
+
+    for copy in d_halos:
+        copy.wait()
+    halo_unpack(place, d_pad, d_rows_in, d_cols_in, d_corners_in)
+    depthwise(d_pad, taps, conv, True)
+    for half in range(2):
+        lanes = slice(half * HALF, (half + 1) * HALF)
+        grad_field[:, :, lanes] = (cotangent[:, :, lanes].astype(F32) + conv[half]).astype(BF16)
+    grad_store = pltpu.make_async_copy(grad_field, grad_hbm, store.at[1])
+    grad_store.start()
+
+    def pack(out, first, total):
+        for to in range(8):
+            for half in range(2):
+                at = first + half * 2
+                out[to, at : at + 2, :] = total[2 * to : 2 * to + 2, half * HALF : (half + 1) * HALF]
+
+    pack(z_out, 4, collect(y_copies, y_out[place.y_lo, place.y_hi].astype(F32), y_in))
+    z_copies = spread(z_in, z_send, z_recv, z, N_Z, place.on_z, lambda to: z_out.at[to])
 
     wait_slots(sz_a, s4_send.at[0], s4_recv.at[0], z, N_Z, place.on_z)
     wait_slots(sy_b, s4_send.at[1], s4_recv.at[1], y, N_Y, place.on_y)
@@ -421,14 +423,6 @@
             sx.at[core, x], sx.at[core, x], sx_send.at[c, k], sx_recv.at[core, x], place.on_x(k, c)
         ).start()
 
-    def pack(out, first, total):
-        for to in range(8):
-            for half in range(2):
-                at = first + half * 2
-                out[to, at : at + 2, :] = total[2 * to : 2 * to + 2, half * HALF : (half + 1) * HALF]
-
-    pack(z_out, 4, collect(y_copies, y_out[place.y_lo, place.y_hi].astype(F32), y_in))
-    z_copies = spread(z_in, z_send, z_recv, z, N_Z, place.on_z, lambda to: z_out.at[to])
     pack(yz_out, 0, collect(zy_copies, zy_out[z].astype(F32), zy_in))
     yz_copies = spread(yz_in, yz_send, yz_recv, y, N_Y, place.on_y, lambda to: yz_out.at[to])
 
@@ -534,8 +528,8 @@
         pltpu.VMEM((N_Z, 16, CH), BF16),
         pltpu.VMEM((N_Y, 16, CH), BF16),
         dma((8,)), dma((8,)), dma((8,)), dma((8,)),
-        dma((2, CHUNKS)), dma((2, CHUNKS)),
-        dma((2, N_X - 1, 2)), dma((2, N_X - 1, 2)),
+        dma((2,)), dma((2,)),
+        dma((2, N_X - 1)), dma((2, N_X - 1)),
         dma((N_Y - 1,)), dma((N_Y - 1,)), dma((N_Z - 1,)), dma((N_Z - 1,)),
         dma((N_Z - 1,)), dma((N_Z - 1,)), dma((N_Y - 1,)), dma((N_Y - 1,)),
         dma, dma,

time: 50.8 us -> 48.2 us (0.949)
  the two profiles are of different devices: /device:TPU:8 before, /device:TPU:1 now
where the time goes in v3:
time: 48.2 us; the launch traced here: 47.9 us
  Pallas kernels  47.3 us (98%)
  between operations  0.64 us (1%)
    pallas_call x1, Pallas kernels, local(): pl.pallas_call(step, out_shape=(grid_shape, grid_shape, jax.ShapeDtypeStr...  45.5 us
    pallas_call x1, Pallas kernels, local(): pl.pallas_call(finish, out_shape=(grid_shape, grid_shape, jax.ShapeDtypeS...  1.77 us

profile of v3, /device:TPU:1, one launch (start us, length us, event | category | flops | bytes accessed | tf_op | source)
XLA Modules:
  0.0 47.9 jit_solution(10545753913073281599)
XLA Ops:
  0.6 45.5 %block_step.1 = (bf16[8,32,256]{2,1,0:T(8,128)(2,1)}, bf16[8,32,256]{2,1,0:T(8,128)(2,1)}, f32[64,256]{1,0:T(8,128)}, f32[8,128]{1,0:T(8,128)}) custom-call(bf16[8,32,256]{2,1,0:T(8,128)(2,1)} %field_hbm.1, f32[7,7,256]{2,1,0:T(8,128)} %taps_hbm.1, f32[1,256]{1,0:T(1,128)} %bitcast.8, bf16[256,1024]{1,0:T(8,128)(2,1)} %w_in_hbm.1, f32[1,1024]{1,0:T(1,128)} %bitcast.7, ...), custom_call_target="tpu_custom_call" | custom-call | tf_op jit(solution)/shard_map/block_step/pallas_call | solution.py:540
  46.2 1.8 %write_outputs.1 = (bf16[8,32,256]{2,1,0:T(8,128)(2,1)}, bf16[8,32,256]{2,1,0:T(8,128)(2,1)}, f32[7,7,256]{2,1,0:T(8,128)}, f32[1,256]{1,0:T(1,128)}, f32[2,256]...) custom-call(bf16[8,32,256]{2,1,0:T(8,128)(2,1)} %get-tuple-element.20.block_in, ...), custom_call_target="tpu_custom_call" | custom-call | tf_op jit(solution)/shard_map/write_outputs/pallas_call | solution.py:559

commit v4 on v3

--- a/solution.py
+++ b/solution.py
@@ -334,13 +334,13 @@
     for copy in d_halos:
         copy.start()
 
-    x_copies_in = send_on_x(0, core_in)
     s_core.wait()
     total = (sums_out[core].astype(F32) + sums_in[...].astype(F32)).astype(BF16)
     sy_a[y] = total[0:16]
     sz_b[z] = total[16:32]
     share(sy_a, s3_send.at[0], s3_recv.at[0], y, N_Y, place.on_y)
     share(sz_b, s3_send.at[1], s3_recv.at[1], z, N_Z, place.on_z)
+    x_copies_in = send_on_x(0, core_in)
 
     block_out[...] = (
         field[...].reshape(CELLS, CH).astype(F32) + layer_scale[...] * branch[...]
@@ -377,6 +377,13 @@
         y_in, y_send, y_recv, y, N_Y, place.on_y,
         lambda to: y_out.at[lax.rem(to, 2), to // 2],
     )
+    wait_slots(sy_a, s3_send.at[0], s3_recv.at[0], y, N_Y, place.on_y)
+    sz_a[z] = gather_sum(sy_a, N_Y).astype(BF16)
+    share(sz_a, s4_send.at[0], s4_recv.at[0], z, N_Z, place.on_z)
+    wait_slots(sz_b, s3_send.at[1], s3_recv.at[1], z, N_Z, place.on_z)
+    sy_b[y] = gather_sum(sz_b, N_Z).astype(BF16)
+    share(sy_b, s4_send.at[1], s4_recv.at[1], y, N_Y, place.on_y)
+
     total = sum_on_x(0, x_copies_in).reshape(2, 4, 16, CH)
     for on_y in range(N_Y):
         for on_z in range(N_Z):
@@ -385,13 +392,6 @@
     zy_copies = spread(
         zy_in, zy_send, zy_recv, z, N_Z, place.on_z, lambda to: zy_out.at[to]
     )
-
-    wait_slots(sy_a, s3_send.at[0], s3_recv.at[0], y, N_Y, place.on_y)
-    sz_a[z] = gather_sum(sy_a, N_Y).astype(BF16)
-    share(sz_a, s4_send.at[0], s4_recv.at[0], z, N_Z, place.on_z)
-    wait_slots(sz_b, s3_send.at[1], s3_recv.at[1], z, N_Z, place.on_z)
-    sy_b[y] = gather_sum(sz_b, N_Z).astype(BF16)
-    share(sy_b, s4_send.at[1], s4_recv.at[1], y, N_Y, place.on_y)
 
     for copy in d_halos:
         copy.wait()

time: 48.2 us -> 46.3 us (0.961)
  Pallas kernels: 47.3 us -> 45.5 us
    pallas_call x1, Pallas kernels: 45.5 us -> 43.7 us  [local(): pl.pallas_call(step, out_shape=(grid_shape, grid_shape, jax.ShapeDtypeStr...]
where the time goes in v4:
time: 46.3 us; the launch traced here: 46.2 us
  Pallas kernels  45.5 us (98%)
  between operations  0.64 us (1%)
    pallas_call x1, Pallas kernels, local(): pl.pallas_call(step, out_shape=(grid_shape, grid_shape, jax.ShapeDtypeStr...  43.7 us
    pallas_call x1, Pallas kernels, local(): pl.pallas_call(finish, out_shape=(grid_shape, grid_shape, jax.ShapeDtypeS...  1.77 us

profile of v4, /device:TPU:1, one launch (start us, length us, event | category | flops | bytes accessed | tf_op | source)
XLA Modules:
  0.0 46.2 jit_solution(15452557786245080250)
XLA Ops:
  0.6 43.7 %block_step.1 = (bf16[8,32,256]{2,1,0:T(8,128)(2,1)}, bf16[8,32,256]{2,1,0:T(8,128)(2,1)}, f32[64,256]{1,0:T(8,128)}, f32[8,128]{1,0:T(8,128)}) custom-call(bf16[8,32,256]{2,1,0:T(8,128)(2,1)} %field_hbm.1, f32[7,7,256]{2,1,0:T(8,128)} %taps_hbm.1, f32[1,256]{1,0:T(1,128)} %bitcast.8, bf16[256,1024]{1,0:T(8,128)(2,1)} %w_in_hbm.1, f32[1,1024]{1,0:T(1,128)} %bitcast.7, ...), custom_call_target="tpu_custom_call" | custom-call | tf_op jit(solution)/shard_map/block_step/pallas_call | solution.py:540
  44.4 1.8 %write_outputs.1 = (bf16[8,32,256]{2,1,0:T(8,128)(2,1)}, bf16[8,32,256]{2,1,0:T(8,128)(2,1)}, f32[7,7,256]{2,1,0:T(8,128)}, f32[1,256]{1,0:T(1,128)}, f32[2,256]...) custom-call(bf16[8,32,256]{2,1,0:T(8,128)(2,1)} %get-tuple-element.20.block_in, ...), custom_call_target="tpu_custom_call" | custom-call | tf_op jit(solution)/shard_map/write_outputs/pallas_call | solution.py:559

commit v5 on v4

--- a/solution.py
+++ b/solution.py
@@ -215,6 +215,12 @@
     for copy in halos[::-1]:
         copy.start()
 
+    pending = []
+
+    def arrived(copy):
+        copy.wait_recv()
+        pending.append(copy)
+
     for copy in loads[1:]:
         copy.wait()
     wide_cot = cotangent[...].reshape(CELLS, CH).astype(F32)
@@ -226,7 +232,7 @@
     sums[55:64, :] = jnp.zeros((9, CH), F32)
 
     for copy in halos:
-        copy.wait()
+        arrived(copy)
     halo_unpack(place, pad, rows_in, cols_in, corners_in)
 
     depthwise(pad, taps, conv, False)
@@ -251,7 +257,7 @@
         return copy
 
     def send_on_x(which, core_copy):
-        core_copy.wait()
+        arrived(core_copy)
         both = part[which, :, :, core].astype(F32) + part_in[which].astype(F32)
         x_out[which] = both.astype(BF16).reshape(2, N_X, 64, CH)
         copies = []
@@ -311,7 +317,7 @@
     def wait_slots(slots, send, recv, own, count, device_on):
         for k in range(1, count):
             other = lax.rem(own + k, count)
-            remote(slots.at[own], slots.at[other], send.at[other], recv.at[other], device_on(other)).wait()
+            arrived(remote(slots.at[own], slots.at[other], send.at[other], recv.at[other], device_on(other)))
 
     def share(slots, send, recv, own, count, device_on):
         for k in range(1, count):
@@ -334,7 +340,7 @@
     for copy in d_halos:
         copy.start()
 
-    s_core.wait()
+    arrived(s_core)
     total = (sums_out[core].astype(F32) + sums_in[...].astype(F32)).astype(BF16)
     sy_a[y] = total[0:16]
     sz_b[z] = total[16:32]
@@ -350,7 +356,7 @@
 
     def sum_on_x(which, copies):
         for copy in copies:
-            copy.wait()
+            arrived(copy)
         total = x_out[which, :, x].astype(F32)
         for k in range(1, N_X):
             total = total + x_in[which, k - 1].astype(F32)
@@ -367,7 +373,7 @@
 
     def collect(copies, total, into):
         for copy in copies:
-            copy.wait()
+            arrived(copy)
         for at in range(len(copies)):
             total = total + into[at].astype(F32)
         return total
@@ -394,7 +400,7 @@
     )
 
     for copy in d_halos:
-        copy.wait()
+        arrived(copy)
     halo_unpack(place, d_pad, d_rows_in, d_cols_in, d_corners_in)
     depthwise(d_pad, taps, conv, True)
     for half in range(2):
@@ -426,16 +432,21 @@
     pack(yz_out, 0, collect(zy_copies, zy_out[z].astype(F32), zy_in))
     yz_copies = spread(yz_in, yz_send, yz_recv, y, N_Y, place.on_y, lambda to: yz_out.at[to])
 
+    while pending:
+        pending.pop().wait_send()
+
     for c, k in last:
         c, k = lax.rem(core + c, 2), lax.rem(x + k, N_X)
-        remote(
-            sx.at[core, x], sx.at[c, k], sx_send.at[c, k], sx_recv.at[c, k], place.on_x(k, c)
-        ).wait()
+        arrived(
+            remote(sx.at[core, x], sx.at[c, k], sx_send.at[c, k], sx_recv.at[c, k], place.on_x(k, c))
+        )
     for c in range(2):
         small_out[c * (SUMS // 2) : (c + 1) * (SUMS // 2), :] = gather_sum(sx.at[c], N_X) * FACTOR
 
     large_out[4:8, :] = collect(z_copies, z_out[z], z_in)[4:8] * FACTOR
     large_out[0:4, :] = collect(yz_copies, yz_out[y], yz_in)[0:4] * FACTOR
+    while pending:
+        pending.pop().wait_send()
     block_store.wait()
     grad_store.wait()
 

time: 46.3 us -> 46.3 us (level)
  no operation moved by 1% of the time
where the time goes in v5:
time: 46.3 us; the launch traced here: 46.2 us
  Pallas kernels  45.5 us (98%)
  between operations  0.64 us (1%)
    pallas_call x1, Pallas kernels, local(): pl.pallas_call(step, out_shape=(grid_shape, grid_shape, jax.ShapeDtypeStr...  43.8 us
    pallas_call x1, Pallas kernels, local(): pl.pallas_call(finish, out_shape=(grid_shape, grid_shape, jax.ShapeDtypeS...  1.77 us

profile of v5, /device:TPU:1, one launch (start us, length us, event | category | flops | bytes accessed | tf_op | source)
XLA Modules:
  0.0 46.2 jit_solution(13434622704738655166)
XLA Ops:
  0.6 43.8 %block_step.1 = (bf16[8,32,256]{2,1,0:T(8,128)(2,1)}, bf16[8,32,256]{2,1,0:T(8,128)(2,1)}, f32[64,256]{1,0:T(8,128)}, f32[8,128]{1,0:T(8,128)}) custom-call(bf16[8,32,256]{2,1,0:T(8,128)(2,1)} %field_hbm.1, f32[7,7,256]{2,1,0:T(8,128)} %taps_hbm.1, f32[1,256]{1,0:T(1,128)} %bitcast.8, bf16[256,1024]{1,0:T(8,128)(2,1)} %w_in_hbm.1, f32[1,1024]{1,0:T(1,128)} %bitcast.7, ...), custom_call_target="tpu_custom_call" | custom-call | tf_op jit(solution)/shard_map/block_step/pallas_call | solution.py:551
  44.4 1.8 %write_outputs.1 = (bf16[8,32,256]{2,1,0:T(8,128)(2,1)}, bf16[8,32,256]{2,1,0:T(8,128)(2,1)}, f32[7,7,256]{2,1,0:T(8,128)}, f32[1,256]{1,0:T(1,128)}, f32[2,256]...) custom-call(bf16[8,32,256]{2,1,0:T(8,128)(2,1)} %get-tuple-element.20.block_in, ...), custom_call_target="tpu_custom_call" | custom-call | tf_op jit(solution)/shard_map/write_outputs/pallas_call | solution.py:570
